TPU v7x, 512 devices: a whole 4x4x16 slice. The times are simulated.
512 devices in a mesh: lon: 64 (over z, y), lat: 4 (over x_lo, core), lev: 2 (over x_hi).
Axes of the slice: x: 4 (x_hi: 2, x_lo: 2; x = x_hi * 2 + x_lo), y: 4, z: 16, core: 2. Of those that a mesh axis runs over, the one named last changes fastest.
Arguments:
- adjoint_in: float32 [32, 96, 8192], P('lev', 'lat', 'lon'), may hold values from -6 to 6
- cotangent: float32 [32, 96, 8192], P('lev', 'lat', 'lon'), may hold values from -3 to 5
- fraction: float32 [3, 32, 96, 8192], P(None, 'lev', 'lat', 'lon'), may hold values from 0 to 1
- base_index: int32 [32, 96, 8192], P('lev', 'lat', 'lon'), may hold values from 0 to 1523, as said below
- block_shift: int32 [2, 32, 96, 64], P(None, 'lev', 'lat', 'lon'), may hold values from -2 to 2, as said below
Outputs:
- adjoint_out: float32 [32, 96, 8192], P('lev', 'lat', 'lon')
Inputs may be any that keep to these rules, and one draw needn't show every extreme that they name: `base_index`: an entry is e * 381 + c with level offset e from 0 to 3 and longitude position c from 0 to 380. `block_shift`: entry [0, l, J, b] is a longitude block offset of magnitude at most ((J // 24 + 1) * 2) // 4; entry [1, l, J, b] is a row offset from -2 to 1.
All inputs are finite; a program needn't handle non-finite values.
Results may differ from a plain program's by a relative error of at most 0.000054.
Values sent between devices are 32-bit elements; how exact they have to be, the bound alone decides.
No kernel may reach another device: no remote copies, remote signals or barrier semaphores. Data moves between devices by JAX's collectives and lax.ppermute only.
A program may use at most 64 MiB of HBM per device.

v0:
```python
import jax
import jax.numpy as jnp
from jax import lax
from jax.sharding import PartitionSpec as P

KREACH = 3


def padded(cells, sides, width):
    for axis, dim in sides:
        count = lax.axis_size(axis)
        ends = count - 1
        head = lax.slice_in_dim(cells, 0, width, axis=dim)
        tail = lax.slice_in_dim(cells, cells.shape[dim] - width, cells.shape[dim], axis=dim)
        cells = jnp.concatenate(
            [
                lax.ppermute(tail, axis, [(i, (i + 1) % count) for i in range(ends)]),
                cells,
                lax.ppermute(head, axis, [((i + 1) % count, i) for i in range(ends)]),
            ],
            axis=dim,
        )
    return cells


def passed_along(value, axis, steps):
    count = lax.axis_size(axis)
    pairs = [(source, (source + steps) % count) for source in range(count)]
    return lax.ppermute(value, axis, pairs)


def lagrange(fraction_part):
    less_one = fraction_part - 1.0
    less_two = fraction_part - 2.0
    plus_one = fraction_part + 1.0
    return (
        -fraction_part * less_one * less_two / 6.0,
        plus_one * less_one * less_two / 2.0,
        -plus_one * fraction_part * less_two / 2.0,
        plus_one * fraction_part * less_one / 6.0,
    )


def fold_axis(field_part, axis_index, inner_size):
    low_part = lax.slice_in_dim(field_part, 0, 3, axis=axis_index)
    middle = lax.slice_in_dim(field_part, 6, 6 + inner_size, axis=axis_index)
    high_part = lax.slice_in_dim(field_part, inner_size + 9, inner_size + 12, axis=axis_index)
    low_pads = [(0, 0)] * field_part.ndim
    low_pads[axis_index] = (0, inner_size - 3)
    high_pads = [(0, 0)] * field_part.ndim
    high_pads[axis_index] = (inner_size - 3, 0)
    return middle + jnp.pad(low_part, low_pads) + jnp.pad(high_part, high_pads)


def fold_rims(field_part, level_count, row_count):
    extended = padded(field_part, (("lat", 1), ("lev", 0)), 3)
    return fold_axis(fold_axis(extended, 0, level_count), 1, row_count)


def return_blocks(blocks, reach_blocks):
    summed = blocks[:, :, reach_blocks]
    for distance in list(range(1, reach_blocks + 1)) + list(range(-reach_blocks, 0)):
        summed = summed + passed_along(blocks[:, :, reach_blocks + distance], "lon", distance)
    return summed


def local(adjoint_in, cotangent, fraction, base_index, block_shift):
    level_count, row_count, column_count = cotangent.shape
    reach_blocks = KREACH
    span_blocks = 2 * reach_blocks + 1
    stride = 3 * column_count - 3
    column_grid = lax.broadcasted_iota(jnp.int32, (1, 1, 3 * column_count), 2)
    level_grid = lax.broadcasted_iota(jnp.int32, (1, 7, 1), 1)
    row_grid = lax.broadcasted_iota(jnp.int32, (row_count, 1), 0)
    tap_grid = lax.broadcasted_iota(jnp.int32, (1, 4), 1)
    unit_grid = lax.broadcasted_iota(jnp.int32, (1, 3), 1)
    target_rows = lax.broadcasted_iota(jnp.int32, (1, 1, row_count + 6), 2)
    target_blocks = lax.broadcasted_iota(jnp.int32, (1, 1, span_blocks), 2)

    def level_step(level_index, buffer_sum):
        vector = lax.dynamic_index_in_dim(cotangent, level_index, 0, keepdims=False)
        fraction_level = lax.dynamic_index_in_dim(fraction, level_index, 1, keepdims=False)
        base_level = lax.dynamic_index_in_dim(base_index, level_index, 0, keepdims=False)
        shifts = lax.dynamic_index_in_dim(block_shift, level_index, 1, keepdims=False)
        level_offset = base_level // stride
        column_offset = base_level - level_offset * stride
        weights_level = lagrange(fraction_level[0])
        weights_row = lagrange(fraction_level[1])
        weights_column = lagrange(fraction_level[2])
        spread = jnp.zeros((row_count, 7, column_count), jnp.float32)
        for level_tap in range(4):
            spread = spread + jnp.where(
                level_offset[:, None, :] + level_tap == level_grid,
                weights_level[level_tap][:, None, :],
                0.0,
            )
        scaled = vector[:, None, :] * spread
        combined = jnp.stack(
            [scaled * weights_row[row_tap][:, None, :] for row_tap in range(4)], axis=2
        )
        combined = combined.reshape(row_count, 28, column_count)
        band_matrix = jnp.zeros((row_count, column_count, 3 * column_count), jnp.float32)
        for column_tap in range(4):
            band_matrix = band_matrix + jnp.where(
                column_offset[:, :, None] + column_tap == column_grid,
                weights_column[column_tap][:, :, None],
                0.0,
            )
        spread_cells = jnp.einsum(
            "rci,rix->rcx",
            combined,
            band_matrix,
            precision=lax.Precision.HIGHEST,
            preferred_element_type=jnp.float32,
        )
        spread_taps = spread_cells.reshape(row_count, 7, 4, 3, column_count)
        target_row = row_grid + shifts[1] + 2 + tap_grid
        target_block = shifts[0] - 1 + reach_blocks + unit_grid
        row_hits = (target_row[:, :, None] == target_rows).astype(jnp.float32)
        block_hits = (target_block[:, :, None] == target_blocks).astype(jnp.float32)
        selector = row_hits[:, :, None, :, None] * block_hits[:, None, :, None, :]
        placed = jnp.einsum(
            "rltux,rtuab->labx",
            spread_taps,
            selector,
            precision=lax.Precision.HIGHEST,
            preferred_element_type=jnp.float32,
        )
        window = lax.dynamic_slice_in_dim(buffer_sum, level_index, 7, 0)
        return lax.dynamic_update_slice_in_dim(buffer_sum, window + placed, level_index, 0)

    empty_sum = jnp.zeros((level_count + 6, row_count + 6, span_blocks, column_count), jnp.float32)
    buffer_sum = lax.fori_loop(0, level_count, level_step, empty_sum)
    collected = fold_rims(return_blocks(buffer_sum, reach_blocks), level_count, row_count)
    return adjoint_in + collected


def solution(mesh):
    return jax.shard_map(
        local,
        mesh=mesh,
        in_specs=(
            P("lev", "lat", "lon"),
            P("lev", "lat", "lon"),
            P(None, "lev", "lat", "lon"),
            P("lev", "lat", "lon"),
            P(None, "lev", "lat", "lon"),
        ),
        out_specs=P("lev", "lat", "lon"),
        check_vma=False,
    )
```

profile of v0, /device:TPU:17, one launch (start us, length us, event | category | flops | bytes accessed | tf_op | source)
XLA Modules:
  0.0 390.8 jit_solution(7232131693305118743)
XLA Ops:
  1.8 311.0 %while.20 = (s32[]{:T(128)}, f32[22,30,7,128]{3,1,0,2:T(8,128)}, s32[2,16,24,1]{2,3,1,0:T(1,128)}, f32[16,24,128]{2,1,0:T(8,128)}, s32[16,24,128]{2,1,0:T(8,128)...) while((s32[]{:T(128)}, f32[22,30,7,128]{3,1,0,2:T(8,128)}, ...), condition=%wide.region_1.2_spmd.clone.clone, body=%wide.region_0.1_spmd.clone.clone.sunk | while | flops 1060682368 | bytes 7754721 | solution.py:133
  4.8 10.1 %fusion.96 = f32[24,28,384]{2,1,0:T(8,128)S(1)} fusion(f32[24,128]{1,0:T(8,128)S(1)} %get-tuple-element.639, s32[24,128]{1,0:T(8,128)S(1)} %get-tuple-element.642, f32[24,128]{1,0:T(8,128)S(1)} %get-tuple-element.643, s32[24,128]{1,0:T(8,128)S(1)} %get-tuple-element.644, f32[24,128]{1,0:T(8,128)S(1)} %get-tuple-element.645, ...), kind=kOutput, calls=%fused_computation.11.clone.1 | convolution fusion | flops 409337856 | bytes 1474560 | tf_op jit(solution)/shard_map/while/body/eval_jaxpr/rci,rix->rcx/dot_general | solution.py:109
  16.8 4.4 %fusion.101 = f32[22,30,7,128]{3,1,0,2:T(8,128)} fusion(f32[22,30,7,128]{3,1,0,2:T(8,128)} %get-tuple-element.674, s32[]{:T(128)} %get-tuple-element.673, f32[24,7,4,3,128]{4,3,2,1,0:T(4,128)S(1)} %reshape.690, f32[24,3,7]{0,1,2:T(4,128)S(1)} %fusion.98, f32[24,4,30]{2,0,1:T(8,128)S(1)} %fusion.100), kind=kOutput, calls=%fused_computation.30.clone.1 | convolution fusion | flops 650529600 | bytes 2651872 | tf_op jit(solution)/shard_map/while/body/eval_jaxpr/rltux,rtuab->labx/dot_general | solution.py:122
  24.3 10.1 %fusion.96 = f32[24,28,384]{2,1,0:T(8,128)S(1)} fusion(f32[24,128]{1,0:T(8,128)S(1)} %get-tuple-element.639, s32[24,128]{1,0:T(8,128)S(1)} %get-tuple-element.642, f32[24,128]{1,0:T(8,128)S(1)} %get-tuple-element.643, s32[24,128]{1,0:T(8,128)S(1)} %get-tuple-element.644, f32[24,128]{1,0:T(8,128)S(1)} %get-tuple-element.645, ...), kind=kOutput, calls=%fused_computation.11.clone.1 | convolution fusion | flops 409337856 | bytes 1474560 | tf_op jit(solution)/shard_map/while/body/eval_jaxpr/rci,rix->rcx/dot_general | solution.py:109
  36.2 4.4 %fusion.101 = f32[22,30,7,128]{3,1,0,2:T(8,128)} fusion(f32[22,30,7,128]{3,1,0,2:T(8,128)} %get-tuple-element.674, s32[]{:T(128)} %get-tuple-element.673, f32[24,7,4,3,128]{4,3,2,1,0:T(4,128)S(1)} %reshape.690, f32[24,3,7]{0,1,2:T(4,128)S(1)} %fusion.98, f32[24,4,30]{2,0,1:T(8,128)S(1)} %fusion.100), kind=kOutput, calls=%fused_computation.30.clone.1 | convolution fusion | flops 650529600 | bytes 2651872 | tf_op jit(solution)/shard_map/while/body/eval_jaxpr/rltux,rtuab->labx/dot_general | solution.py:122
  43.7 10.1 %fusion.96 = f32[24,28,384]{2,1,0:T(8,128)S(1)} fusion(f32[24,128]{1,0:T(8,128)S(1)} %get-tuple-element.639, s32[24,128]{1,0:T(8,128)S(1)} %get-tuple-element.642, f32[24,128]{1,0:T(8,128)S(1)} %get-tuple-element.643, s32[24,128]{1,0:T(8,128)S(1)} %get-tuple-element.644, f32[24,128]{1,0:T(8,128)S(1)} %get-tuple-element.645, ...), kind=kOutput, calls=%fused_computation.11.clone.1 | convolution fusion | flops 409337856 | bytes 1474560 | tf_op jit(solution)/shard_map/while/body/eval_jaxpr/rci,rix->rcx/dot_general | solution.py:109
  55.7 4.4 %fusion.101 = f32[22,30,7,128]{3,1,0,2:T(8,128)} fusion(f32[22,30,7,128]{3,1,0,2:T(8,128)} %get-tuple-element.674, s32[]{:T(128)} %get-tuple-element.673, f32[24,7,4,3,128]{4,3,2,1,0:T(4,128)S(1)} %reshape.690, f32[24,3,7]{0,1,2:T(4,128)S(1)} %fusion.98, f32[24,4,30]{2,0,1:T(8,128)S(1)} %fusion.100), kind=kOutput, calls=%fused_computation.30.clone.1 | convolution fusion | flops 650529600 | bytes 2651872 | tf_op jit(solution)/shard_map/while/body/eval_jaxpr/rltux,rtuab->labx/dot_general | solution.py:122
  63.1 10.1 %fusion.96 = f32[24,28,384]{2,1,0:T(8,128)S(1)} fusion(f32[24,128]{1,0:T(8,128)S(1)} %get-tuple-element.639, s32[24,128]{1,0:T(8,128)S(1)} %get-tuple-element.642, f32[24,128]{1,0:T(8,128)S(1)} %get-tuple-element.643, s32[24,128]{1,0:T(8,128)S(1)} %get-tuple-element.644, f32[24,128]{1,0:T(8,128)S(1)} %get-tuple-element.645, ...), kind=kOutput, calls=%fused_computation.11.clone.1 | convolution fusion | flops 409337856 | bytes 1474560 | tf_op jit(solution)/shard_map/while/body/eval_jaxpr/rci,rix->rcx/dot_general | solution.py:109
  82.6 10.1 %fusion.96 = f32[24,28,384]{2,1,0:T(8,128)S(1)} fusion(f32[24,128]{1,0:T(8,128)S(1)} %get-tuple-element.639, s32[24,128]{1,0:T(8,128)S(1)} %get-tuple-element.642, f32[24,128]{1,0:T(8,128)S(1)} %get-tuple-element.643, s32[24,128]{1,0:T(8,128)S(1)} %get-tuple-element.644, f32[24,128]{1,0:T(8,128)S(1)} %get-tuple-element.645, ...), kind=kOutput, calls=%fused_computation.11.clone.1 | convolution fusion | flops 409337856 | bytes 1474560 | tf_op jit(solution)/shard_map/while/body/eval_jaxpr/rci,rix->rcx/dot_general | solution.py:109
  102.0 10.1 %fusion.96 = f32[24,28,384]{2,1,0:T(8,128)S(1)} fusion(f32[24,128]{1,0:T(8,128)S(1)} %get-tuple-element.639, s32[24,128]{1,0:T(8,128)S(1)} %get-tuple-element.642, f32[24,128]{1,0:T(8,128)S(1)} %get-tuple-element.643, s32[24,128]{1,0:T(8,128)S(1)} %get-tuple-element.644, f32[24,128]{1,0:T(8,128)S(1)} %get-tuple-element.645, ...), kind=kOutput, calls=%fused_computation.11.clone.1 | convolution fusion | flops 409337856 | bytes 1474560 | tf_op jit(solution)/shard_map/while/body/eval_jaxpr/rci,rix->rcx/dot_general | solution.py:109
  121.4 10.1 %fusion.96 = f32[24,28,384]{2,1,0:T(8,128)S(1)} fusion(f32[24,128]{1,0:T(8,128)S(1)} %get-tuple-element.639, s32[24,128]{1,0:T(8,128)S(1)} %get-tuple-element.642, f32[24,128]{1,0:T(8,128)S(1)} %get-tuple-element.643, s32[24,128]{1,0:T(8,128)S(1)} %get-tuple-element.644, f32[24,128]{1,0:T(8,128)S(1)} %get-tuple-element.645, ...), kind=kOutput, calls=%fused_computation.11.clone.1 | convolution fusion | flops 409337856 | bytes 1474560 | tf_op jit(solution)/shard_map/while/body/eval_jaxpr/rci,rix->rcx/dot_general | solution.py:109
  140.8 10.1 %fusion.96 = f32[24,28,384]{2,1,0:T(8,128)S(1)} fusion(f32[24,128]{1,0:T(8,128)S(1)} %get-tuple-element.639, s32[24,128]{1,0:T(8,128)S(1)} %get-tuple-element.642, f32[24,128]{1,0:T(8,128)S(1)} %get-tuple-element.643, s32[24,128]{1,0:T(8,128)S(1)} %get-tuple-element.644, f32[24,128]{1,0:T(8,128)S(1)} %get-tuple-element.645, ...), kind=kOutput, calls=%fused_computation.11.clone.1 | convolution fusion | flops 409337856 | bytes 1474560 | tf_op jit(solution)/shard_map/while/body/eval_jaxpr/rci,rix->rcx/dot_general | solution.py:109
  152.8 4.4 %fusion.101 = f32[22,30,7,128]{3,1,0,2:T(8,128)} fusion(f32[22,30,7,128]{3,1,0,2:T(8,128)} %get-tuple-element.674, s32[]{:T(128)} %get-tuple-element.673, f32[24,7,4,3,128]{4,3,2,1,0:T(4,128)S(1)} %reshape.690, f32[24,3,7]{0,1,2:T(4,128)S(1)} %fusion.98, f32[24,4,30]{2,0,1:T(8,128)S(1)} %fusion.100), kind=kOutput, calls=%fused_computation.30.clone.1 | convolution fusion | flops 650529600 | bytes 2651872 | tf_op jit(solution)/shard_map/while/body/eval_jaxpr/rltux,rtuab->labx/dot_general | solution.py:122
  160.3 10.1 %fusion.96 = f32[24,28,384]{2,1,0:T(8,128)S(1)} fusion(f32[24,128]{1,0:T(8,128)S(1)} %get-tuple-element.639, s32[24,128]{1,0:T(8,128)S(1)} %get-tuple-element.642, f32[24,128]{1,0:T(8,128)S(1)} %get-tuple-element.643, s32[24,128]{1,0:T(8,128)S(1)} %get-tuple-element.644, f32[24,128]{1,0:T(8,128)S(1)} %get-tuple-element.645, ...), kind=kOutput, calls=%fused_computation.11.clone.1 | convolution fusion | flops 409337856 | bytes 1474560 | tf_op jit(solution)/shard_map/while/body/eval_jaxpr/rci,rix->rcx/dot_general | solution.py:109
  172.3 4.4 %fusion.101 = f32[22,30,7,128]{3,1,0,2:T(8,128)} fusion(f32[22,30,7,128]{3,1,0,2:T(8,128)} %get-tuple-element.674, s32[]{:T(128)} %get-tuple-element.673, f32[24,7,4,3,128]{4,3,2,1,0:T(4,128)S(1)} %reshape.690, f32[24,3,7]{0,1,2:T(4,128)S(1)} %fusion.98, f32[24,4,30]{2,0,1:T(8,128)S(1)} %fusion.100), kind=kOutput, calls=%fused_computation.30.clone.1 | convolution fusion | flops 650529600 | bytes 2651872 | tf_op jit(solution)/shard_map/while/body/eval_jaxpr/rltux,rtuab->labx/dot_general | solution.py:122
  179.7 10.1 %fusion.96 = f32[24,28,384]{2,1,0:T(8,128)S(1)} fusion(f32[24,128]{1,0:T(8,128)S(1)} %get-tuple-element.639, s32[24,128]{1,0:T(8,128)S(1)} %get-tuple-element.642, f32[24,128]{1,0:T(8,128)S(1)} %get-tuple-element.643, s32[24,128]{1,0:T(8,128)S(1)} %get-tuple-element.644, f32[24,128]{1,0:T(8,128)S(1)} %get-tuple-element.645, ...), kind=kOutput, calls=%fused_computation.11.clone.1 | convolution fusion | flops 409337856 | bytes 1474560 | tf_op jit(solution)/shard_map/while/body/eval_jaxpr/rci,rix->rcx/dot_general | solution.py:109
  191.7 4.4 %fusion.101 = f32[22,30,7,128]{3,1,0,2:T(8,128)} fusion(f32[22,30,7,128]{3,1,0,2:T(8,128)} %get-tuple-element.674, s32[]{:T(128)} %get-tuple-element.673, f32[24,7,4,3,128]{4,3,2,1,0:T(4,128)S(1)} %reshape.690, f32[24,3,7]{0,1,2:T(4,128)S(1)} %fusion.98, f32[24,4,30]{2,0,1:T(8,128)S(1)} %fusion.100), kind=kOutput, calls=%fused_computation.30.clone.1 | convolution fusion | flops 650529600 | bytes 2651872 | tf_op jit(solution)/shard_map/while/body/eval_jaxpr/rltux,rtuab->labx/dot_general | solution.py:122
  199.2 10.1 %fusion.96 = f32[24,28,384]{2,1,0:T(8,128)S(1)} fusion(f32[24,128]{1,0:T(8,128)S(1)} %get-tuple-element.639, s32[24,128]{1,0:T(8,128)S(1)} %get-tuple-element.642, f32[24,128]{1,0:T(8,128)S(1)} %get-tuple-element.643, s32[24,128]{1,0:T(8,128)S(1)} %get-tuple-element.644, f32[24,128]{1,0:T(8,128)S(1)} %get-tuple-element.645, ...), kind=kOutput, calls=%fused_computation.11.clone.1 | convolution fusion | flops 409337856 | bytes 1474560 | tf_op jit(solution)/shard_map/while/body/eval_jaxpr/rci,rix->rcx/dot_general | solution.py:109
  211.1 4.4 %fusion.101 = f32[22,30,7,128]{3,1,0,2:T(8,128)} fusion(f32[22,30,7,128]{3,1,0,2:T(8,128)} %get-tuple-element.674, s32[]{:T(128)} %get-tuple-element.673, f32[24,7,4,3,128]{4,3,2,1,0:T(4,128)S(1)} %reshape.690, f32[24,3,7]{0,1,2:T(4,128)S(1)} %fusion.98, f32[24,4,30]{2,0,1:T(8,128)S(1)} %fusion.100), kind=kOutput, calls=%fused_computation.30.clone.1 | convolution fusion | flops 650529600 | bytes 2651872 | tf_op jit(solution)/shard_map/while/body/eval_jaxpr/rltux,rtuab->labx/dot_general | solution.py:122
  218.6 10.1 %fusion.96 = f32[24,28,384]{2,1,0:T(8,128)S(1)} fusion(f32[24,128]{1,0:T(8,128)S(1)} %get-tuple-element.639, s32[24,128]{1,0:T(8,128)S(1)} %get-tuple-element.642, f32[24,128]{1,0:T(8,128)S(1)} %get-tuple-element.643, s32[24,128]{1,0:T(8,128)S(1)} %get-tuple-element.644, f32[24,128]{1,0:T(8,128)S(1)} %get-tuple-element.645, ...), kind=kOutput, calls=%fused_computation.11.clone.1 | convolution fusion | flops 409337856 | bytes 1474560 | tf_op jit(solution)/shard_map/while/body/eval_jaxpr/rci,rix->rcx/dot_general | solution.py:109
  238.0 10.1 %fusion.96 = f32[24,28,384]{2,1,0:T(8,128)S(1)} fusion(f32[24,128]{1,0:T(8,128)S(1)} %get-tuple-element.639, s32[24,128]{1,0:T(8,128)S(1)} %get-tuple-element.642, f32[24,128]{1,0:T(8,128)S(1)} %get-tuple-element.643, s32[24,128]{1,0:T(8,128)S(1)} %get-tuple-element.644, f32[24,128]{1,0:T(8,128)S(1)} %get-tuple-element.645, ...), kind=kOutput, calls=%fused_computation.11.clone.1 | convolution fusion | flops 409337856 | bytes 1474560 | tf_op jit(solution)/shard_map/while/body/eval_jaxpr/rci,rix->rcx/dot_general | solution.py:109
  250.0 4.4 %fusion.101 = f32[22,30,7,128]{3,1,0,2:T(8,128)} fusion(f32[22,30,7,128]{3,1,0,2:T(8,128)} %get-tuple-element.674, s32[]{:T(128)} %get-tuple-element.673, f32[24,7,4,3,128]{4,3,2,1,0:T(4,128)S(1)} %reshape.690, f32[24,3,7]{0,1,2:T(4,128)S(1)} %fusion.98, f32[24,4,30]{2,0,1:T(8,128)S(1)} %fusion.100), kind=kOutput, calls=%fused_computation.30.clone.1 | convolution fusion | flops 650529600 | bytes 2651872 | tf_op jit(solution)/shard_map/while/body/eval_jaxpr/rltux,rtuab->labx/dot_general | solution.py:122
  257.5 10.1 %fusion.96 = f32[24,28,384]{2,1,0:T(8,128)S(1)} fusion(f32[24,128]{1,0:T(8,128)S(1)} %get-tuple-element.639, s32[24,128]{1,0:T(8,128)S(1)} %get-tuple-element.642, f32[24,128]{1,0:T(8,128)S(1)} %get-tuple-element.643, s32[24,128]{1,0:T(8,128)S(1)} %get-tuple-element.644, f32[24,128]{1,0:T(8,128)S(1)} %get-tuple-element.645, ...), kind=kOutput, calls=%fused_computation.11.clone.1 | convolution fusion | flops 409337856 | bytes 1474560 | tf_op jit(solution)/shard_map/while/body/eval_jaxpr/rci,rix->rcx/dot_general | solution.py:109
  269.5 4.4 %fusion.101 = f32[22,30,7,128]{3,1,0,2:T(8,128)} fusion(f32[22,30,7,128]{3,1,0,2:T(8,128)} %get-tuple-element.674, s32[]{:T(128)} %get-tuple-element.673, f32[24,7,4,3,128]{4,3,2,1,0:T(4,128)S(1)} %reshape.690, f32[24,3,7]{0,1,2:T(4,128)S(1)} %fusion.98, f32[24,4,30]{2,0,1:T(8,128)S(1)} %fusion.100), kind=kOutput, calls=%fused_computation.30.clone.1 | convolution fusion | flops 650529600 | bytes 2651872 | tf_op jit(solution)/shard_map/while/body/eval_jaxpr/rltux,rtuab->labx/dot_general | solution.py:122
  276.9 10.1 %fusion.96 = f32[24,28,384]{2,1,0:T(8,128)S(1)} fusion(f32[24,128]{1,0:T(8,128)S(1)} %get-tuple-element.639, s32[24,128]{1,0:T(8,128)S(1)} %get-tuple-element.642, f32[24,128]{1,0:T(8,128)S(1)} %get-tuple-element.643, s32[24,128]{1,0:T(8,128)S(1)} %get-tuple-element.644, f32[24,128]{1,0:T(8,128)S(1)} %get-tuple-element.645, ...), kind=kOutput, calls=%fused_computation.11.clone.1 | convolution fusion | flops 409337856 | bytes 1474560 | tf_op jit(solution)/shard_map/while/body/eval_jaxpr/rci,rix->rcx/dot_general | solution.py:109
  288.9 4.4 %fusion.101 = f32[22,30,7,128]{3,1,0,2:T(8,128)} fusion(f32[22,30,7,128]{3,1,0,2:T(8,128)} %get-tuple-element.674, s32[]{:T(128)} %get-tuple-element.673, f32[24,7,4,3,128]{4,3,2,1,0:T(4,128)S(1)} %reshape.690, f32[24,3,7]{0,1,2:T(4,128)S(1)} %fusion.98, f32[24,4,30]{2,0,1:T(8,128)S(1)} %fusion.100), kind=kOutput, calls=%fused_computation.30.clone.1 | convolution fusion | flops 650529600 | bytes 2651872 | tf_op jit(solution)/shard_map/while/body/eval_jaxpr/rltux,rtuab->labx/dot_general | solution.py:122
  296.4 10.1 %fusion.96 = f32[24,28,384]{2,1,0:T(8,128)S(1)} fusion(f32[24,128]{1,0:T(8,128)S(1)} %get-tuple-element.639, s32[24,128]{1,0:T(8,128)S(1)} %get-tuple-element.642, f32[24,128]{1,0:T(8,128)S(1)} %get-tuple-element.643, s32[24,128]{1,0:T(8,128)S(1)} %get-tuple-element.644, f32[24,128]{1,0:T(8,128)S(1)} %get-tuple-element.645, ...), kind=kOutput, calls=%fused_computation.11.clone.1 | convolution fusion | flops 409337856 | bytes 1474560 | tf_op jit(solution)/shard_map/while/body/eval_jaxpr/rci,rix->rcx/dot_general | solution.py:109
  325.1 7.0 %collective-permute-start.3 = (f32[22,30,128]{2,1,0:T(8,128)S(1)}, f32[22,30,128]{2,1,0:T(8,128)S(1)}, u32[]{:S(2)}, u32[]{:S(2)}) collective-permute-start(f32[22,30,128]{2,1,0:T(8,128)S(1)} %get-tuple-element.569), channel_id=1, source_target_pairs={{0,488},{8,496},{16,504},{24,0},{32,8},{40,16},{48,24},{56,32},{64... | collective-permute-start | bytes 1013768 | tf_op jit(solution)/shard_map/ppermute | solution.py:29
  336.5 4.7 %collective-permute-start.5 = (f32[22,30,128]{2,1,0:T(8,128)S(1)}, f32[22,30,128]{2,1,0:T(8,128)S(1)}, u32[]{:S(2)}, u32[]{:S(2)}) collective-permute-start(f32[22,30,128]{2,1,0:T(8,128)S(1)} %get-tuple-element.572), channel_id=1, source_target_pairs={{0,504},{8,0},{16,8},{24,16},{32,24},{40,32},{48,40},{56,48},{64,5... | collective-permute-start | bytes 1013768 | tf_op jit(solution)/shard_map/ppermute | solution.py:29
  341.2 11.5 %collective-permute-done.2 = f32[22,30,128]{2,1,0:T(8,128)S(1)} collective-permute-done((f32[22,30,128]{2,1,0:T(8,128)S(1)}, f32[22,30,128]{2,1,0:T(8,128)S(1)}, u32[]{:S(2)}, u32[]{:S(2)}) %collective-permute-start.2) | collective-permute-done | bytes 337952 | tf_op jit(solution)/shard_map/ppermute | solution.py:29
  352.7 16.2 %collective-permute-done.5 = f32[22,30,128]{2,1,0:T(8,128)S(1)} collective-permute-done((f32[22,30,128]{2,1,0:T(8,128)S(1)}, f32[22,30,128]{2,1,0:T(8,128)S(1)}, u32[]{:S(2)}, u32[]{:S(2)}) %collective-permute-start.5) | collective-permute-done | bytes 337952 | tf_op jit(solution)/shard_map/ppermute | solution.py:29
  384.8 5.1 %collective-permute-done.9 = f32[3,36,128]{2,1,0:T(8,128)S(1)} collective-permute-done((f32[3,36,128]{2,1,0:T(8,128)S(1)}, f32[3,36,128]{2,1,0:T(8,128)S(1)}, u32[]{:S(2)}, u32[]{:S(2)}) %collective-permute-start.9) | collective-permute-done | bytes 55328 | tf_op jit(solution)/shard_map/ppermute | solution.py:19
  (258 shorter events, 139.0 us)
Async XLA Ops:
  314.5 21.9 %collective-permute-start = (f32[22,30,128]{2,1,0:T(8,128)S(1)}, f32[22,30,128]{2,1,0:T(8,128)S(1)}, u32[]{:S(2)}, u32[]{:S(2)}) collective-permute-start(f32[22,30,128]{2,1,0:T(8,128)S(1)} %get-tuple-element.568), channel_id=1, source_target_pairs={{0,8},{8,16},{16,24},{24,32},{32,40},{40,48},{48,56},{56,64},{64,7... | collective-permute-start | bytes 1013768 | tf_op jit(solution)/shard_map/ppermute | solution.py:29
  317.5 23.7 %collective-permute-start.1 = (f32[22,30,128]{2,1,0:T(8,128)S(1)}, f32[22,30,128]{2,1,0:T(8,128)S(1)}, u32[]{:S(2)}, u32[]{:S(2)}) collective-permute-start(f32[22,30,128]{2,1,0:T(8,128)S(1)} %get-tuple-element.571), channel_id=1, source_target_pairs={{0,16},{8,24},{16,32},{24,40},{32,48},{40,56},{48,64},{56,72},{64,... | collective-permute-start | bytes 1013768 | tf_op jit(solution)/shard_map/ppermute | solution.py:29
  321.1 31.7 %collective-permute-start.2 = (f32[22,30,128]{2,1,0:T(8,128)S(1)}, f32[22,30,128]{2,1,0:T(8,128)S(1)}, u32[]{:S(2)}, u32[]{:S(2)}) collective-permute-start(f32[22,30,128]{2,1,0:T(8,128)S(1)} %get-tuple-element.570), channel_id=1, source_target_pairs={{0,24},{8,32},{16,40},{24,48},{32,56},{40,64},{48,72},{56,80},{64,... | collective-permute-start | bytes 1013768 | tf_op jit(solution)/shard_map/ppermute | solution.py:29
  325.1 27.6 %collective-permute-start.3 = (f32[22,30,128]{2,1,0:T(8,128)S(1)}, f32[22,30,128]{2,1,0:T(8,128)S(1)}, u32[]{:S(2)}, u32[]{:S(2)}) collective-permute-start(f32[22,30,128]{2,1,0:T(8,128)S(1)} %get-tuple-element.569), channel_id=1, source_target_pairs={{0,488},{8,496},{16,504},{24,0},{32,8},{40,16},{48,24},{56,32},{64... | collective-permute-start | bytes 1013768 | tf_op jit(solution)/shard_map/ppermute | solution.py:29
  332.2 20.6 %collective-permute-start.4 = (f32[22,30,128]{2,1,0:T(8,128)S(1)}, f32[22,30,128]{2,1,0:T(8,128)S(1)}, u32[]{:S(2)}, u32[]{:S(2)}) collective-permute-start(f32[22,30,128]{2,1,0:T(8,128)S(1)} %get-tuple-element.573), channel_id=1, source_target_pairs={{0,496},{8,504},{16,0},{24,8},{32,16},{40,24},{48,32},{56,40},{64,... | collective-permute-start | bytes 1013768 | tf_op jit(solution)/shard_map/ppermute | solution.py:29
  336.4 53.6 %copy-start = (f32[16,24,128]{2,1,0:T(8,128)S(1)}, f32[16,24,128]{2,1,0:T(8,128)}, u32[]{:S(2)}) copy-start(f32[16,24,128]{2,1,0:T(8,128)} %param.7) | copy-start | bytes 589828
  336.5 53.5 %copy-start.1 = (pred[24]{0:T(512)(128)(4,1)S(1)}, pred[24]{0:T(512)(128)(4,1)}, u32[]{:S(2)}) copy-start(pred[24]{0:T(512)(128)(4,1)} %constant.244.clone.1) | copy-start | bytes 76
  336.5 32.5 %collective-permute-start.5 = (f32[22,30,128]{2,1,0:T(8,128)S(1)}, f32[22,30,128]{2,1,0:T(8,128)S(1)}, u32[]{:S(2)}, u32[]{:S(2)}) collective-permute-start(f32[22,30,128]{2,1,0:T(8,128)S(1)} %get-tuple-element.572), channel_id=1, source_target_pairs={{0,504},{8,0},{16,8},{24,16},{32,24},{40,32},{48,40},{56,48},{64,5... | collective-permute-start | bytes 1013768 | tf_op jit(solution)/shard_map/ppermute | solution.py:29
  370.2 5.4 %collective-permute-start.6 = (f32[22,3,128]{2,1,0:T(4,128)S(1)}, f32[22,3,128]{2,1,0:T(4,128)S(1)}, u32[]{:S(2)}, u32[]{:S(2)}) collective-permute-start(f32[22,3,128]{2,1,0:T(4,128)S(1)} %get-tuple-element.576), channel_id=1, source_target_pairs={{0,2},{2,4},{4,6},{1,3},{3,5},{5,7},{8,10},{10,12},{12,14},{9,11},... | collective-permute-start | bytes 101384 | tf_op jit(solution)/shard_map/ppermute | solution.py:17
  373.7 5.4 %collective-permute-start.7 = (f32[22,3,128]{2,1,0:T(4,128)S(1)}, f32[22,3,128]{2,1,0:T(4,128)S(1)}, u32[]{:S(2)}, u32[]{:S(2)}) collective-permute-start(f32[22,3,128]{2,1,0:T(4,128)S(1)} %get-tuple-element.577), channel_id=1, source_target_pairs={{2,0},{4,2},{6,4},{3,1},{5,3},{7,5},{10,8},{12,10},{14,12},{11,9},... | collective-permute-start | bytes 101384 | tf_op jit(solution)/shard_map/ppermute | solution.py:19
  379.1 5.7 %collective-permute-start.8 = (f32[3,36,128]{2,1,0:T(8,128)S(1)}, f32[3,36,128]{2,1,0:T(8,128)S(1)}, u32[]{:S(2)}, u32[]{:S(2)}) collective-permute-start(f32[3,36,128]{2,1,0:T(8,128)S(1)} %get-tuple-element.574), channel_id=1, source_target_pairs={{0,1},{2,3},{4,5},{6,7},{8,9},{10,11},{12,13},{14,15},{16,17},{18,... | collective-permute-start | bytes 165896 | tf_op jit(solution)/shard_map/ppermute | solution.py:17
  383.5 6.5 %collective-permute-start.9 = (f32[3,36,128]{2,1,0:T(8,128)S(1)}, f32[3,36,128]{2,1,0:T(8,128)S(1)}, u32[]{:S(2)}, u32[]{:S(2)}) collective-permute-start(f32[3,36,128]{2,1,0:T(8,128)S(1)} %get-tuple-element.575), channel_id=1, source_target_pairs={{1,0},{3,2},{5,4},{7,6},{9,8},{11,10},{13,12},{15,14},{17,16},{19,... | collective-permute-start | bytes 165896 | tf_op jit(solution)/shard_map/ppermute | solution.py:19
where the time goes:
time: 397 us; the launch traced here: 391 us
  matrix products  233 us (59%)
  other arithmetic  61.6 us (16%)
  starting transfers between devices  37.6 us (9%)
  waiting for transfers between devices  36.3 us (9%)
  local copies, waits for them, and re-layouts  21.7 us (5%)
    dot_general x16, matrix products, level_step(): jnp.einsum('rci,rix->rcx', combined, band_matrix, precision=lax.Precision...  162 us
    dot_general x16, matrix products, level_step(): jnp.einsum('rltux,rtuab->labx', spread_taps, selector, precision=lax.Prec...  70.7 us
    ppermute x6, waiting for transfers between devices, passed_along(): return lax.ppermute(value, axis, pairs)  27.7 us
    ppermute x6, starting transfers between devices, passed_along(): return lax.ppermute(value, axis, pairs)  26.6 us
    div x16, other arithmetic, lagrange(): -fraction_part * less_one * less_two / 6.0  12.2 us
    add x32, other arithmetic, level_step(): column_offset[:, :, None] + column_tap == column_grid  11.6 us
    add x16, other arithmetic, level_step(): level_offset[:, None, :] + level_tap == level_grid  11.5 us
    mul x16, local copies, waits for them, and re-layouts, level_step(): scaled = vector[:, None, :] * spread  11.4 us
  transfers between devices with their start and end apart: 10, of which 4 were waited for; matrix products, arithmetic and copies ran while one was open for 0% of the time, Pallas kernels for 0%

commit v1 on v0

v1 whole, which is shorter than its diff:
```python
import functools

import jax
import jax.numpy as jnp
from jax import lax
from jax.experimental import pallas as pl
from jax.experimental.pallas import tpu as pltpu
from jax.sharding import PartitionSpec as P

KREACH = 3
SPAN = 2 * KREACH + 1
HALO = 3
AXES = ("lon", "lat", "lev")
F32 = jnp.float32
BF16 = jnp.bfloat16


def lagrange(f):
    m1 = f - 1.0
    m2 = f - 2.0
    p1 = f + 1.0
    return (
        -f * m1 * m2 / 6.0,
        p1 * m1 * m2 / 2.0,
        -p1 * f * m2 / 2.0,
        p1 * f * m1 / 6.0,
    )


class Sizes:
    def __init__(self, levels, rows, cols):
        self.levels, self.rows, self.cols = levels, rows, cols
        self.nr = rows + 2 * HALO
        self.nl = -(-(levels + 2 * HALO + 1) // 8) * 8
        self.total = SPAN * self.nr * self.nl
        self.points = levels * rows


def prepare(sz, cot_ref, frac_ref, base_ref, pos_ref, wl_ref, wr_ref, wc_ref):
    stride = 3 * sz.cols - 3

    def body(l, carry):
        rows = pl.ds(pl.multiple_of(l * sz.rows, 8), sz.rows)
        base = base_ref[l]
        e = jnp.zeros_like(base)
        for cut in range(1, 4):
            e = e + (base >= cut * stride).astype(jnp.int32)
        c = base - e * stride
        q = c // sz.cols
        r = c - q * sz.cols
        pos_ref[0, rows] = e.astype(F32)
        pos_ref[1, rows] = q.astype(F32)
        pos_ref[2, rows] = r.astype(F32)
        cot = cot_ref[l]
        for t, w in enumerate(lagrange(frac_ref[0, l])):
            wl_ref[t, rows] = cot * w
        for t, w in enumerate(lagrange(frac_ref[1, l])):
            wr_ref[t, rows] = w
        for t, w in enumerate(lagrange(frac_ref[2, l])):
            high = w.astype(BF16).astype(F32)
            wc_ref[t, rows] = high
            wc_ref[4 + t, rows] = w - high
        return carry

    lax.fori_loop(0, sz.levels, body, 0)


def block_terms(sz, l, j, shift_ref, pos_ref, wl_ref, wr_ref, wc_ref):
    cols = sz.cols
    point = l * sz.rows + j

    def row(ref, t, n):
        return jnp.broadcast_to(ref[t, pl.ds(point, 1), :], (n, cols))

    def row16(ref, t):
        return row(ref, t, 16).astype(BF16)

    k8 = lax.broadcasted_iota(jnp.int32, (8, cols), 0).astype(F32)
    x16 = lax.broadcasted_iota(jnp.int32, (16, cols), 0).astype(F32).astype(BF16)
    z16 = jnp.zeros((16, cols), BF16)
    d = k8 - row(pos_ref, 0, 8)
    spread = jnp.zeros((8, cols), F32)
    for t in range(4):
        spread = jnp.where(d == float(t), row(wl_ref, t, 8), spread)
    term = jnp.concatenate([spread * row(wr_ref, t, 8) for t in range(4)], 0)
    high = term.astype(BF16)
    low = (term - high.astype(F32)).astype(BF16)
    q = row16(pos_ref, 1)
    q = jnp.concatenate([q, q], 0)
    z32 = jnp.zeros((32, cols), BF16)
    lh = jnp.concatenate([jnp.where(q == BF16(u), high, z32) for u in range(3)], 0)
    ll = jnp.concatenate([jnp.where(q == BF16(u), low, z32) for u in range(3)], 0)
    lhs = jnp.concatenate(
        [jnp.concatenate([lh, lh], 1), jnp.concatenate([ll, ll], 1)], 0
    )
    offset = x16 - row16(pos_ref, 2)
    wh = [row16(wc_ref, t) for t in range(4)]
    wl = [row16(wc_ref, 4 + t) for t in range(4)]
    bh, bl = [], []
    for tile in range(cols // 16 + 1):
        at = offset + BF16(16.0 * tile)
        a, b = z16, z16
        for t in range(4):
            hit = at == BF16(float(t))
            a = jnp.where(hit, wh[t], a)
            b = jnp.where(hit, wl[t], b)
        bh.append(a)
        bl.append(b)
    rest = [z16] * (cols // 16 - 1)
    band = jnp.concatenate(
        [jnp.concatenate(bh + rest, 0), jnp.concatenate(bl + rest, 0)], 1
    )
    out = lax.dot_general(
        lhs, band, (((1,), (1,)), ((), ())), preferred_element_type=F32
    )
    out = out[:96] + out[96:]
    blocks = shift_ref[l, j]
    shift = shift_ref[sz.levels + l, j]
    start = ((blocks + KREACH - 1) * sz.nr + (j + shift + 2)) * sz.nl + l
    return out[:, :cols], out[:64, cols:], start


def add_blocks(sz, places, acc_ref, *refs):
    results = [block_terms(sz, l, j, *refs) for l, j in places]
    for main, over, start in results:
        for q in range(3):
            for t in range(4):
                v = main[q * 32 + t * 8 : q * 32 + t * 8 + 8]
                if q > 0:
                    v = v + over[(q - 1) * 32 + t * 8 : (q - 1) * 32 + t * 8 + 8]
                at = pl.ds(start + (q * sz.nr + t) * sz.nl, 8)
                acc_ref[at] = acc_ref[at] + v


def clear_kernel(sz, acc_ref):
    zero = jnp.zeros((sz.nl, sz.cols), F32)

    def clear(i, carry):
        acc_ref[pl.ds(pl.multiple_of(i * sz.nl, 8), sz.nl)] = zero
        return carry

    lax.fori_loop(0, SPAN * sz.nr, clear, 0, unroll=6)


def first_kernel(
    sz, shift_ref, acc_in, cot_ref, frac_ref, base_ref,
    acc_ref, pos_ref, wl_ref, wr_ref, wc_ref, down_ref, up_ref,
):
    prepare(sz, cot_ref, frac_ref, base_ref, pos_ref, wl_ref, wr_ref, wc_ref)
    refs = (shift_ref, pos_ref, wl_ref, wr_ref, wc_ref)
    rim = list(range(HALO)) + list(range(sz.rows - HALO, sz.rows))

    def rims(i, carry):
        add_blocks(sz, [(i * 2 + u, j) for u in range(2) for j in rim], acc_ref, *refs)
        return carry

    lax.fori_loop(0, sz.levels // 2, rims, 0)
    edge = jnp.where(lax.axis_index("lev") == 0, sz.levels - HALO, 0)
    inner = range(HALO, sz.rows - HALO)

    def edges(i, carry):
        add_blocks(sz, [(edge + i, j) for j in inner], acc_ref, *refs)
        return carry

    lax.fori_loop(0, HALO, edges, 0)
    n = HALO * sz.nl
    for b in range(SPAN):
        down_ref[b] = acc_ref[pl.ds(b * sz.nr * sz.nl, n)]
        up_ref[b] = acc_ref[pl.ds((b * sz.nr + sz.rows + HALO) * sz.nl, n)]


def inner_kernel(
    sz, lower, upper, shift_ref, acc_in, pos_ref, wl_ref, wr_ref, wc_ref, acc_ref
):
    refs = (shift_ref, pos_ref, wl_ref, wr_ref, wc_ref)
    start = jnp.where(lax.axis_index("lev") == 0, 0, HALO)
    inner = range(HALO, sz.rows - HALO)

    def levels(i, carry):
        add_blocks(sz, [(start + i, j) for j in inner], acc_ref, *refs)
        return carry

    lax.fori_loop(lower, upper, levels, 0)


def row_kernel(sz, acc_in, down_ref, up_ref, acc_ref, out_ref):
    n = HALO * sz.nl
    slot = jnp.where(lax.axis_index("lev") == 0, sz.levels + HALO, 0)
    for b in range(SPAN):
        low = pl.ds((b * sz.nr + HALO) * sz.nl, n)
        high = pl.ds((b * sz.nr + sz.rows) * sz.nl, n)
        acc_ref[low] = acc_ref[low] + up_ref[b]
        acc_ref[high] = acc_ref[high] + down_ref[b]
    for b in range(SPAN):
        for k in range(HALO):
            for g in range(sz.rows // 8):
                at = (b * sz.nr + HALO + 8 * g) * sz.nl + slot + k
                out_ref[b, k, 8 * g : 8 * g + 8] = acc_ref[pl.ds(at, 8, stride=sz.nl)]


def level_kernel(sz, acc_ref, got_ref, *out_refs):
    target = jnp.where(lax.axis_index("lev") == 0, sz.levels - HALO, 0)
    for b in range(SPAN):
        def level(l, carry, b=b):
            for g in range(sz.rows // 8):
                at = (b * sz.nr + HALO + 8 * g) * sz.nl + HALO + l
                out_refs[b][l, 8 * g : 8 * g + 8] = acc_ref[pl.ds(at, 8, stride=sz.nl)]
            return carry

        lax.fori_loop(0, sz.levels, level, 0, unroll=4)
        for k in range(HALO):
            out_refs[b][target + k] = out_refs[b][target + k] + got_ref[b, k]


def call(kernel, out_shape, operands, flops, smem=0, aliases=None):
    vmem = pl.BlockSpec(memory_space=pltpu.VMEM)
    specs = []
    for i in range(len(operands)):
        if i < smem:
            specs.append(pl.BlockSpec(memory_space=pltpu.SMEM))
        else:
            specs.append(vmem)
    return pl.pallas_call(
        kernel,
        out_shape=out_shape,
        in_specs=specs,
        out_specs=jax.tree.map(lambda _: vmem, out_shape),
        input_output_aliases=aliases or {},
        cost_estimate=pl.CostEstimate(flops=flops, bytes_accessed=1 << 20, transcendentals=0),
        compiler_params=pltpu.CompilerParams(vmem_limit_bytes=32 << 20),
    )(*operands)


def shape(*dims):
    return jax.ShapeDtypeStruct(dims, F32)


def permute(value, sizes, step):
    pairs = []
    for lon in range(sizes[0]):
        for lat in range(sizes[1]):
            for lev in range(sizes[2]):
                to = step(lon, lat, lev)
                if to is not None:
                    pairs.append(
                        (
                            (lon * sizes[1] + lat) * sizes[2] + lev,
                            (to[0] * sizes[1] + to[1]) * sizes[2] + to[2],
                        )
                    )
    return lax.ppermute(value, AXES, pairs)


def local(adjoint_in, cotangent, fraction, base_index, block_shift):
    levels, rows, cols = cotangent.shape
    sz = Sizes(levels, rows, cols)
    sizes = tuple(lax.axis_size(axis) for axis in AXES)
    shifts = block_shift.reshape(2 * levels, rows)
    n = sz.points
    work = 2 * 192 * 256 * 256
    acc = call(functools.partial(clear_kernel, sz), shape(sz.total, cols), (), 10 * work)
    acc, pos, wl, wr, wc, down, up = call(
        functools.partial(first_kernel, sz),
        (
            shape(sz.total, cols), shape(3, n, cols), shape(4, n, cols),
            shape(4, n, cols), shape(8, n, cols),
            shape(SPAN, HALO * sz.nl, cols), shape(SPAN, HALO * sz.nl, cols),
        ),
        (shifts, acc, cotangent, fraction, base_index),
        150 * work,
        smem=1,
        aliases={1: 0},
    )

    def rows_by(d):
        def step(lon, lat, lev):
            return (lon, lat + d, lev) if 0 <= lat + d < sizes[1] else None
        return step

    got_down = permute(down, sizes, rows_by(-1))
    got_up = permute(up, sizes, rows_by(1))
    part = 5
    inner_levels = levels - HALO

    def inner(acc, lower, upper):
        return call(
            functools.partial(inner_kernel, sz, lower, upper),
            shape(sz.total, cols),
            (shifts, acc, pos, wl, wr, wc),
            (upper - lower) * 18 * work,
            smem=1,
            aliases={1: 0},
        )

    acc = inner(acc, 0, part)
    acc, edge = call(
        functools.partial(row_kernel, sz),
        (shape(sz.total, cols), shape(SPAN, HALO, rows, cols)),
        (acc, got_down, got_up),
        1 << 20,
        aliases={0: 0},
    )
    got_edge = permute(edge, sizes, lambda lon, lat, lev: (lon, lat, 1 - lev))
    acc = inner(acc, part, inner_levels)
    blocks = call(
        functools.partial(level_kernel, sz),
        tuple(shape(levels, rows, cols) for _ in range(SPAN)),
        (acc, got_edge),
        1 << 20,
    )

    def reach(lat):
        return ((lat + 1) * (KREACH - 1)) // sizes[1] + 1

    def around(d):
        def step(lon, lat, lev):
            far = max(reach(lat), reach(min(lat + 1, sizes[1] - 1)))
            return ((lon + d) % sizes[0], lat, lev) if abs(d) <= far else None

        return step

    total = adjoint_in + blocks[KREACH]
    order = (2, -2, 1, -1, 3, -3)
    got = [permute(blocks[KREACH + d], sizes, around(d)) for d in order]
    for value in got:
        total = total + value
    return total


def solution(mesh):
    return jax.shard_map(
        local,
        mesh=mesh,
        in_specs=(
            P("lev", "lat", "lon"),
            P("lev", "lat", "lon"),
            P(None, "lev", "lat", "lon"),
            P("lev", "lat", "lon"),
            P(None, "lev", "lat", "lon"),
        ),
        out_specs=P("lev", "lat", "lon"),
        check_vma=False,
    )
```

time: 397 us -> 66.7 us (0.17)
  the two profiles are of different devices: /device:TPU:17 before, /device:TPU:2 now
where the time goes in v1:
time: 66.7 us; the launch traced here: 66.3 us
  starting transfers between devices  35.8 us (54%)
  Pallas kernels  18.5 us (28%)
  waiting for transfers between devices  10.1 us (15%)
  local copies, waits for them, and re-layouts  0.98 us (1%)
  other arithmetic  0.78 us (1%)
    ppermute x9, starting transfers between devices, permute(): return lax.ppermute(value, AXES, pairs)  35.8 us
    pallas_call x6, Pallas kernels, call(): pl.pallas_call(kernel, out_shape=out_shape, in_specs=specs, out_specs=jax...  18.5 us
    ppermute x9, waiting for transfers between devices, permute(): return lax.ppermute(value, AXES, pairs)  10.1 us
  transfers between devices with their start and end apart: 9, of which 4 were waited for; matrix products, arithmetic and copies ran while one was open for 0% of the time, Pallas kernels for 15%

profile of v1, /device:TPU:2, one launch (start us, length us, event | category | flops | bytes accessed | tf_op | source)
XLA Modules:
  0.0 66.3 jit_solution(10462293063619864220)
XLA Ops:
  0.0 0.0 copy-start.2
  0.0 0.2 shard_map.55.acc_in
  0.3 0.5 copy-done
  0.7 0.2 copy-done.3
  0.9 0.2 copy-done.1
  1.2 0.0 copy-done.2
  1.2 7.5 %shard_map.56 = (f32[5040,128]{1,0:T(8,128)S(1)}, f32[3,384,128]{2,1,0:T(8,128)S(1)}, f32[4,384,128]{2,1,0:T(8,128)S(1)}, f32[4,384,128]{2,1,0:T(8,128)S(1)}, f3...) custom-call(s32[32,24]{1,0:T(8,128)S(1)} %bitcast.1, ...), custom_call_target="tpu_custom_call", output_to_operand_aliasing={{0}: (1, {})} | custom-call | flops 3774873600 | bytes 1048576 | tf_op jit(solution)/shard_map/pallas_call | solution.py:223
  8.8 1.9 %collective-permute-start = (f32[7,72,128]{2,1,0:T(8,128)S(1)}, f32[7,72,128]{2,1,0:T(8,128)S(1)}, u32[]{:S(2)}, u32[]{:S(2)}) collective-permute-start(f32[7,72,128]{2,1,0:T(8,128)S(1)} %get-tuple-element.26), channel_id=1, source_target_pairs={{2,0},{3,1},{4,2},{5,3},{6,4},{7,5},{10,8},{11,9},{12,10},{13,11},... | collective-permute-start | bytes 774152 | tf_op jit(solution)/shard_map/ppermute | solution.py:251
  10.7 2.4 %collective-permute-start.1 = (f32[7,72,128]{2,1,0:T(8,128)S(1)}, f32[7,72,128]{2,1,0:T(8,128)S(1)}, u32[]{:S(2)}, u32[]{:S(2)}) collective-permute-start(f32[7,72,128]{2,1,0:T(8,128)S(1)} %get-tuple-element.27), channel_id=1, source_target_pairs={{0,2},{1,3},{2,4},{3,5},{4,6},{5,7},{8,10},{9,11},{10,12},{11,13},... | collective-permute-start | bytes 774152 | tf_op jit(solution)/shard_map/ppermute | solution.py:251
  13.1 4.1 %shard_map.57.acc_in = f32[5040,128]{1,0:T(8,128)S(1)} custom-call(s32[32,24]{1,0:T(8,128)S(1)} %bitcast.2, f32[5040,128]{1,0:T(8,128)S(1)} %get-tuple-element.21.acc_in, f32[3,384,128]{2,1,0:T(8,128)S(1)} %get-tuple-element.22.pos_ref, f32[4,384,128]{2,1,0:T(8,128)S(1)} %get-tuple-element.23.wl_ref, ...), custom_call_target="tpu_custom_call", output_to_operand_aliasing={{}: (1, {})} | custom-call | flops 2264924160 | bytes 1048576 | tf_op jit(solution)/shard_map/pallas_call | solution.py:223
  17.3 0.0 collective-permute-done.down_ref
  17.3 5.3 %collective-permute-done.1.up_ref = f32[7,72,128]{2,1,0:T(8,128)S(1)} collective-permute-done((f32[7,72,128]{2,1,0:T(8,128)S(1)}, f32[7,72,128]{2,1,0:T(8,128)S(1)}, u32[]{:S(2)}, u32[]{:S(2)}) %collective-permute-start.1) | collective-permute-done | bytes 258080 | tf_op jit(solution)/shard_map/ppermute | solution.py:251
  22.6 0.1 shard_map.58
  22.7 1.9 %collective-permute-start.2 = (f32[7,3,24,128]{3,2,1,0:T(8,128)S(1)}, f32[7,3,24,128]{3,2,1,0:T(8,128)S(1)}, u32[]{:S(2)}, u32[]{:S(2)}) collective-permute-start(f32[7,3,24,128]{3,2,1,0:T(8,128)S(1)} %get-tuple-element.29), channel_id=1, source_target_pairs={{0,1},{1,0},{2,3},{3,2},{4,5},{5,4},{6,7},{7,6},{8,9},{9,8},{10,11... | collective-permute-start | bytes 774152 | tf_op jit(solution)/shard_map/ppermute | solution.py:251
  24.6 6.1 %shard_map.59.acc_ref = f32[5040,128]{1,0:T(8,128)S(1)} custom-call(s32[32,24]{1,0:T(8,128)S(1)} %bitcast.3, f32[5040,128]{1,0:T(8,128)S(1)} %get-tuple-element.28.acc_in, f32[3,384,128]{2,1,0:T(8,128)S(1)} %get-tuple-element.22.pos_ref, f32[4,384,128]{2,1,0:T(8,128)S(1)} %get-tuple-element.23.wl_ref, ...), custom_call_target="tpu_custom_call", output_to_operand_aliasing={{}: (1, {})} | custom-call | flops 3623878656 | bytes 1048576 | tf_op jit(solution)/shard_map/pallas_call | solution.py:223
  30.8 0.0 copy-start.4
  30.8 1.7 %collective-permute-done.2.got_ref = f32[7,3,24,128]{3,2,1,0:T(8,128)S(1)} collective-permute-done((f32[7,3,24,128]{3,2,1,0:T(8,128)S(1)}, f32[7,3,24,128]{3,2,1,0:T(8,128)S(1)}, u32[]{:S(2)}, u32[]{:S(2)}) %collective-permute-start.2) | collective-permute-done | bytes 258080 | tf_op jit(solution)/shard_map/ppermute | solution.py:251
  32.4 0.3 shard_map.60
  32.8 1.9 %collective-permute-start.3 = (f32[16,24,128]{2,1,0:T(8,128)S(1)}, f32[16,24,128]{2,1,0:T(8,128)S(1)}, u32[]{:S(2)}, u32[]{:S(2)}) collective-permute-start(f32[16,24,128]{2,1,0:T(8,128)S(1)} %get-tuple-element.31), channel_id=1, source_target_pairs={{0,16},{1,17},{2,18},{3,19},{4,20},{5,21},{6,22},{7,23},{8,24},{9,... | collective-permute-start | bytes 589832 | tf_op jit(solution)/shard_map/ppermute | solution.py:251
  34.7 10.5 %collective-permute-start.4 = (f32[16,24,128]{2,1,0:T(8,128)S(1)}, f32[16,24,128]{2,1,0:T(8,128)S(1)}, u32[]{:S(2)}, u32[]{:S(2)}) collective-permute-start(f32[16,24,128]{2,1,0:T(8,128)S(1)} %get-tuple-element.32), channel_id=1, source_target_pairs={{0,496},{1,497},{2,498},{3,499},{4,500},{5,501},{6,502},{7,503},{8... | collective-permute-start | bytes 589832 | tf_op jit(solution)/shard_map/ppermute | solution.py:251
  45.2 2.6 %collective-permute-start.5 = (f32[16,24,128]{2,1,0:T(8,128)S(1)}, f32[16,24,128]{2,1,0:T(8,128)S(1)}, u32[]{:S(2)}, u32[]{:S(2)}) collective-permute-start(f32[16,24,128]{2,1,0:T(8,128)S(1)} %get-tuple-element.33), channel_id=1, source_target_pairs={{0,8},{1,9},{2,10},{3,11},{4,12},{5,13},{6,14},{7,15},{8,16},{9,17... | collective-permute-start | bytes 589832 | tf_op jit(solution)/shard_map/ppermute | solution.py:251
  47.9 6.5 %collective-permute-start.6 = (f32[16,24,128]{2,1,0:T(8,128)S(1)}, f32[16,24,128]{2,1,0:T(8,128)S(1)}, u32[]{:S(2)}, u32[]{:S(2)}) collective-permute-start(f32[16,24,128]{2,1,0:T(8,128)S(1)} %get-tuple-element.34), channel_id=1, source_target_pairs={{0,504},{1,505},{2,506},{3,507},{4,508},{5,509},{6,510},{7,511},{8... | collective-permute-start | bytes 589832 | tf_op jit(solution)/shard_map/ppermute | solution.py:251
  54.4 1.9 %collective-permute-start.7 = (f32[16,24,128]{2,1,0:T(8,128)S(1)}, f32[16,24,128]{2,1,0:T(8,128)S(1)}, u32[]{:S(2)}, u32[]{:S(2)}) collective-permute-start(f32[16,24,128]{2,1,0:T(8,128)S(1)} %get-tuple-element.35), channel_id=1, source_target_pairs={{4,28},{5,29},{6,30},{7,31},{12,36},{13,37},{14,38},{15,39},{20,44... | collective-permute-start | bytes 589832 | tf_op jit(solution)/shard_map/ppermute | solution.py:251
  56.3 0.0 collective-permute-done.3
  56.3 6.0 %collective-permute-start.8 = (f32[16,24,128]{2,1,0:T(8,128)S(1)}, f32[16,24,128]{2,1,0:T(8,128)S(1)}, u32[]{:S(2)}, u32[]{:S(2)}) collective-permute-start(f32[16,24,128]{2,1,0:T(8,128)S(1)} %get-tuple-element.36), channel_id=1, source_target_pairs={{4,492},{5,493},{6,494},{7,495},{12,500},{13,501},{14,502},{15,503... | collective-permute-start | bytes 589832 | tf_op jit(solution)/shard_map/ppermute | solution.py:251
  62.4 0.0 collective-permute-done.4
  62.4 0.0 collective-permute-done.5
  62.4 0.0 collective-permute-done.6
  62.4 1.7 %collective-permute-done.7 = f32[16,24,128]{2,1,0:T(8,128)S(1)} collective-permute-done((f32[16,24,128]{2,1,0:T(8,128)S(1)}, f32[16,24,128]{2,1,0:T(8,128)S(1)}, u32[]{:S(2)}, u32[]{:S(2)}) %collective-permute-start.7) | collective-permute-done | bytes 196640 | tf_op jit(solution)/shard_map/ppermute | solution.py:251
  64.1 1.5 %collective-permute-done.8 = f32[16,24,128]{2,1,0:T(8,128)S(1)} collective-permute-done((f32[16,24,128]{2,1,0:T(8,128)S(1)}, f32[16,24,128]{2,1,0:T(8,128)S(1)}, u32[]{:S(2)}, u32[]{:S(2)}) %collective-permute-start.8) | collective-permute-done | bytes 196640 | tf_op jit(solution)/shard_map/ppermute | solution.py:251
  65.5 0.0 copy-done.4
  65.5 0.8 %add_add_fusion = f32[16,24,128]{2,1,0:T(8,128)} fusion(f32[16,24,128]{2,1,0:T(8,128)S(1)} %collective-permute-done.8, f32[16,24,128]{2,1,0:T(8,128)S(1)} %collective-permute-done.7, f32[16,24,128]{2,1,0:T(8,128)S(1)} %collective-permute-done.6, f32[16,24,128]{2,1,0:T(8,128)S(1)} %collective-permute-done.5, f32[16,24,128]{2,1,0:T(8,128)S(1)} %collective-permute-done.4, ...), kind=kLoop, calls=%fused_computation | loop fusion | flops 344064 | bytes 1769472 | tf_op jit(solution)/shard_map/add | solution.py:326
  (3 shorter events, 0.0 us)
Async XLA Ops:
  0.0 0.7 %copy-start = (s32[2,16,24,1]{2,3,1,0:T(1,128)S(1)}, s32[2,16,24,1]{2,3,1,0:T(1,128)}, u32[]{:S(2)}) copy-start(s32[2,16,24,1]{2,3,1,0:T(1,128)} %param.9) | copy-start | bytes 9220
  0.0 0.9 %copy-start.3 = (s32[16,24,128]{2,1,0:T(8,128)S(1)}, s32[16,24,128]{2,1,0:T(8,128)}, u32[]{:S(2)}) copy-start(s32[16,24,128]{2,1,0:T(8,128)} %base_ref.1) | copy-start | bytes 589828
  0.0 1.2 %copy-start.1 = (f32[3,16,24,128]{3,2,1,0:T(8,128)S(1)}, f32[3,16,24,128]{3,2,1,0:T(8,128)}, u32[]{:S(2)}) copy-start(f32[3,16,24,128]{3,2,1,0:T(8,128)} %frac_ref.1) | copy-start | bytes 1769476
  0.0 1.2 %copy-start.2 = (f32[16,24,128]{2,1,0:T(8,128)S(1)}, f32[16,24,128]{2,1,0:T(8,128)}, u32[]{:S(2)}) copy-start(f32[16,24,128]{2,1,0:T(8,128)} %cot_ref.1) | copy-start | bytes 589828
  8.8 8.5 %collective-permute-start = (f32[7,72,128]{2,1,0:T(8,128)S(1)}, f32[7,72,128]{2,1,0:T(8,128)S(1)}, u32[]{:S(2)}, u32[]{:S(2)}) collective-permute-start(f32[7,72,128]{2,1,0:T(8,128)S(1)} %get-tuple-element.26), channel_id=1, source_target_pairs={{2,0},{3,1},{4,2},{5,3},{6,4},{7,5},{10,8},{11,9},{12,10},{13,11},... | collective-permute-start | bytes 774152 | tf_op jit(solution)/shard_map/ppermute | solution.py:251
  10.7 11.9 %collective-permute-start.1 = (f32[7,72,128]{2,1,0:T(8,128)S(1)}, f32[7,72,128]{2,1,0:T(8,128)S(1)}, u32[]{:S(2)}, u32[]{:S(2)}) collective-permute-start(f32[7,72,128]{2,1,0:T(8,128)S(1)} %get-tuple-element.27), channel_id=1, source_target_pairs={{0,2},{1,3},{2,4},{3,5},{4,6},{5,7},{8,10},{9,11},{10,12},{11,13},... | collective-permute-start | bytes 774152 | tf_op jit(solution)/shard_map/ppermute | solution.py:251
  22.7 9.7 %collective-permute-start.2 = (f32[7,3,24,128]{3,2,1,0:T(8,128)S(1)}, f32[7,3,24,128]{3,2,1,0:T(8,128)S(1)}, u32[]{:S(2)}, u32[]{:S(2)}) collective-permute-start(f32[7,3,24,128]{3,2,1,0:T(8,128)S(1)} %get-tuple-element.29), channel_id=1, source_target_pairs={{0,1},{1,0},{2,3},{3,2},{4,5},{5,4},{6,7},{7,6},{8,9},{9,8},{10,11... | collective-permute-start | bytes 774152 | tf_op jit(solution)/shard_map/ppermute | solution.py:251
  30.8 34.8 %copy-start.4 = (f32[16,24,128]{2,1,0:T(8,128)S(1)}, f32[16,24,128]{2,1,0:T(8,128)}, u32[]{:S(2)}) copy-start(f32[16,24,128]{2,1,0:T(8,128)} %param.5) | copy-start | bytes 589828
  32.8 23.5 %collective-permute-start.3 = (f32[16,24,128]{2,1,0:T(8,128)S(1)}, f32[16,24,128]{2,1,0:T(8,128)S(1)}, u32[]{:S(2)}, u32[]{:S(2)}) collective-permute-start(f32[16,24,128]{2,1,0:T(8,128)S(1)} %get-tuple-element.31), channel_id=1, source_target_pairs={{0,16},{1,17},{2,18},{3,19},{4,20},{5,21},{6,22},{7,23},{8,24},{9,... | collective-permute-start | bytes 589832 | tf_op jit(solution)/shard_map/ppermute | solution.py:251
  34.7 27.7 %collective-permute-start.4 = (f32[16,24,128]{2,1,0:T(8,128)S(1)}, f32[16,24,128]{2,1,0:T(8,128)S(1)}, u32[]{:S(2)}, u32[]{:S(2)}) collective-permute-start(f32[16,24,128]{2,1,0:T(8,128)S(1)} %get-tuple-element.32), channel_id=1, source_target_pairs={{0,496},{1,497},{2,498},{3,499},{4,500},{5,501},{6,502},{7,503},{8... | collective-permute-start | bytes 589832 | tf_op jit(solution)/shard_map/ppermute | solution.py:251
  45.2 17.2 %collective-permute-start.5 = (f32[16,24,128]{2,1,0:T(8,128)S(1)}, f32[16,24,128]{2,1,0:T(8,128)S(1)}, u32[]{:S(2)}, u32[]{:S(2)}) collective-permute-start(f32[16,24,128]{2,1,0:T(8,128)S(1)} %get-tuple-element.33), channel_id=1, source_target_pairs={{0,8},{1,9},{2,10},{3,11},{4,12},{5,13},{6,14},{7,15},{8,16},{9,17... | collective-permute-start | bytes 589832 | tf_op jit(solution)/shard_map/ppermute | solution.py:251
  47.9 14.5 %collective-permute-start.6 = (f32[16,24,128]{2,1,0:T(8,128)S(1)}, f32[16,24,128]{2,1,0:T(8,128)S(1)}, u32[]{:S(2)}, u32[]{:S(2)}) collective-permute-start(f32[16,24,128]{2,1,0:T(8,128)S(1)} %get-tuple-element.34), channel_id=1, source_target_pairs={{0,504},{1,505},{2,506},{3,507},{4,508},{5,509},{6,510},{7,511},{8... | collective-permute-start | bytes 589832 | tf_op jit(solution)/shard_map/ppermute | solution.py:251
  54.4 9.7 %collective-permute-start.7 = (f32[16,24,128]{2,1,0:T(8,128)S(1)}, f32[16,24,128]{2,1,0:T(8,128)S(1)}, u32[]{:S(2)}, u32[]{:S(2)}) collective-permute-start(f32[16,24,128]{2,1,0:T(8,128)S(1)} %get-tuple-element.35), channel_id=1, source_target_pairs={{4,28},{5,29},{6,30},{7,31},{12,36},{13,37},{14,38},{15,39},{20,44... | collective-permute-start | bytes 589832 | tf_op jit(solution)/shard_map/ppermute | solution.py:251
  56.3 9.2 %collective-permute-start.8 = (f32[16,24,128]{2,1,0:T(8,128)S(1)}, f32[16,24,128]{2,1,0:T(8,128)S(1)}, u32[]{:S(2)}, u32[]{:S(2)}) collective-permute-start(f32[16,24,128]{2,1,0:T(8,128)S(1)} %get-tuple-element.36), channel_id=1, source_target_pairs={{4,492},{5,493},{6,494},{7,495},{12,500},{13,501},{14,502},{15,503... | collective-permute-start | bytes 589832 | tf_op jit(solution)/shard_map/ppermute | solution.py:251

commit v2 on v1

--- a/solution.py
+++ b/solution.py
@@ -20,10 +20,10 @@
     m2 = f - 2.0
     p1 = f + 1.0
     return (
-        -f * m1 * m2 / 6.0,
-        p1 * m1 * m2 / 2.0,
-        -p1 * f * m2 / 2.0,
-        p1 * f * m1 / 6.0,
+        -f * m1 * m2 * (1.0 / 6.0),
+        p1 * m1 * m2 * 0.5,
+        -p1 * f * m2 * 0.5,
+        p1 * f * m1 * (1.0 / 6.0),
     )
 
 
@@ -46,11 +46,13 @@
         for cut in range(1, 4):
             e = e + (base >= cut * stride).astype(jnp.int32)
         c = base - e * stride
-        q = c // sz.cols
+        q = (c >= sz.cols).astype(jnp.int32) + (c >= 2 * sz.cols).astype(jnp.int32)
         r = c - q * sz.cols
         pos_ref[0, rows] = e.astype(F32)
         pos_ref[1, rows] = q.astype(F32)
-        pos_ref[2, rows] = r.astype(F32)
+        part = r // 16
+        pos_ref[2, rows] = (r - part * 16).astype(F32)
+        pos_ref[3, rows] = part.astype(F32)
         cot = cot_ref[l]
         for t, w in enumerate(lagrange(frac_ref[0, l])):
             wl_ref[t, rows] = cot * w
@@ -94,18 +96,20 @@
         [jnp.concatenate([lh, lh], 1), jnp.concatenate([ll, ll], 1)], 0
     )
     offset = x16 - row16(pos_ref, 2)
-    wh = [row16(wc_ref, t) for t in range(4)]
-    wl = [row16(wc_ref, 4 + t) for t in range(4)]
+    below = offset < z16
+    part = row16(pos_ref, 3)
+    place = jnp.where(below, part + BF16(1.0), part)
+    tap = jnp.where(below, offset + BF16(16.0), offset)
+    wh, wl = z16, z16
+    for t in range(4):
+        hit = tap == BF16(float(t))
+        wh = jnp.where(hit, row16(wc_ref, t), wh)
+        wl = jnp.where(hit, row16(wc_ref, 4 + t), wl)
     bh, bl = [], []
     for tile in range(cols // 16 + 1):
-        at = offset + BF16(16.0 * tile)
-        a, b = z16, z16
-        for t in range(4):
-            hit = at == BF16(float(t))
-            a = jnp.where(hit, wh[t], a)
-            b = jnp.where(hit, wl[t], b)
-        bh.append(a)
-        bl.append(b)
+        hit = place == BF16(float(tile))
+        bh.append(jnp.where(hit, wh, z16))
+        bl.append(jnp.where(hit, wl, z16))
     rest = [z16] * (cols // 16 - 1)
     band = jnp.concatenate(
         [jnp.concatenate(bh + rest, 0), jnp.concatenate(bl + rest, 0)], 1
@@ -121,8 +125,7 @@
 
 
 def add_blocks(sz, places, acc_ref, *refs):
-    results = [block_terms(sz, l, j, *refs) for l, j in places]
-    for main, over, start in results:
+    def put(main, over, start):
         for q in range(3):
             for t in range(4):
                 v = main[q * 32 + t * 8 : q * 32 + t * 8 + 8]
@@ -131,6 +134,14 @@
                 at = pl.ds(start + (q * sz.nr + t) * sz.nl, 8)
                 acc_ref[at] = acc_ref[at] + v
 
+    waiting = None
+    for l, j in places:
+        found = block_terms(sz, l, j, *refs)
+        if waiting is not None:
+            put(*waiting)
+        waiting = found
+    put(*waiting)
+
 
 def clear_kernel(sz, acc_ref):
     zero = jnp.zeros((sz.nl, sz.cols), F32)
@@ -144,17 +155,17 @@
 
 def first_kernel(
     sz, shift_ref, acc_in, cot_ref, frac_ref, base_ref,
-    acc_ref, pos_ref, wl_ref, wr_ref, wc_ref, down_ref, up_ref,
+    acc_ref, pos_ref, wl_ref, wr_ref, wc_ref, near_ref, far_ref,
 ):
     prepare(sz, cot_ref, frac_ref, base_ref, pos_ref, wl_ref, wr_ref, wc_ref)
     refs = (shift_ref, pos_ref, wl_ref, wr_ref, wc_ref)
     rim = list(range(HALO)) + list(range(sz.rows - HALO, sz.rows))
 
     def rims(i, carry):
-        add_blocks(sz, [(i * 2 + u, j) for u in range(2) for j in rim], acc_ref, *refs)
-        return carry
-
-    lax.fori_loop(0, sz.levels // 2, rims, 0)
+        add_blocks(sz, [(i * 4 + u, j) for u in range(4) for j in rim], acc_ref, *refs)
+        return carry
+
+    lax.fori_loop(0, sz.levels // 4, rims, 0)
     edge = jnp.where(lax.axis_index("lev") == 0, sz.levels - HALO, 0)
     inner = range(HALO, sz.rows - HALO)
 
@@ -164,9 +175,12 @@
 
     lax.fori_loop(0, HALO, edges, 0)
     n = HALO * sz.nl
+    even = lax.axis_index("lat") % 2 == 0
+    near = jnp.where(even, sz.rows + HALO, 0)
+    far = jnp.where(even, 0, sz.rows + HALO)
     for b in range(SPAN):
-        down_ref[b] = acc_ref[pl.ds(b * sz.nr * sz.nl, n)]
-        up_ref[b] = acc_ref[pl.ds((b * sz.nr + sz.rows + HALO) * sz.nl, n)]
+        near_ref[b] = acc_ref[pl.ds((b * sz.nr + near) * sz.nl, n)]
+        far_ref[b] = acc_ref[pl.ds((b * sz.nr + far) * sz.nl, n)]
 
 
 def inner_kernel(
@@ -174,23 +188,27 @@
 ):
     refs = (shift_ref, pos_ref, wl_ref, wr_ref, wc_ref)
     start = jnp.where(lax.axis_index("lev") == 0, 0, HALO)
-    inner = range(HALO, sz.rows - HALO)
-
-    def levels(i, carry):
-        add_blocks(sz, [(start + i, j) for j in inner], acc_ref, *refs)
-        return carry
-
-    lax.fori_loop(lower, upper, levels, 0)
-
-
-def row_kernel(sz, acc_in, down_ref, up_ref, acc_ref, out_ref):
+    span = range(sz.levels - HALO)
+
+    def rows(i, carry):
+        places = [(start + l, HALO * (i + 1) + u) for u in range(HALO) for l in span]
+        add_blocks(sz, places, acc_ref, *refs)
+        return carry
+
+    lax.fori_loop(lower, upper, rows, 0)
+
+
+def row_kernel(sz, acc_in, near_ref, far_ref, acc_ref, out_ref):
     n = HALO * sz.nl
     slot = jnp.where(lax.axis_index("lev") == 0, sz.levels + HALO, 0)
+    even = lax.axis_index("lat") % 2 == 0
+    near_row = jnp.where(even, sz.rows, HALO)
+    far_row = jnp.where(even, HALO, sz.rows)
     for b in range(SPAN):
-        low = pl.ds((b * sz.nr + HALO) * sz.nl, n)
-        high = pl.ds((b * sz.nr + sz.rows) * sz.nl, n)
-        acc_ref[low] = acc_ref[low] + up_ref[b]
-        acc_ref[high] = acc_ref[high] + down_ref[b]
+        near = pl.ds((b * sz.nr + near_row) * sz.nl, n)
+        acc_ref[near] = acc_ref[near] + near_ref[b]
+        far = pl.ds((b * sz.nr + far_row) * sz.nl, n)
+        acc_ref[far] = acc_ref[far] + far_ref[b]
     for b in range(SPAN):
         for k in range(HALO):
             for g in range(sz.rows // 8):
@@ -198,18 +216,33 @@
                 out_ref[b, k, 8 * g : 8 * g + 8] = acc_ref[pl.ds(at, 8, stride=sz.nl)]
 
 
-def level_kernel(sz, acc_ref, got_ref, *out_refs):
+def level_kernel(sz, far_of, acc_ref, got_ref, *refs):
+    out_refs, rim_refs = refs[:SPAN], refs[SPAN:]
     target = jnp.where(lax.axis_index("lev") == 0, sz.levels - HALO, 0)
+
+    def cells(b, l, g):
+        at = (b * sz.nr + HALO + 8 * g) * sz.nl + HALO + l
+        return acc_ref[pl.ds(at, 8, stride=sz.nl)]
+
     for b in range(SPAN):
         def level(l, carry, b=b):
             for g in range(sz.rows // 8):
-                at = (b * sz.nr + HALO + 8 * g) * sz.nl + HALO + l
-                out_refs[b][l, 8 * g : 8 * g + 8] = acc_ref[pl.ds(at, 8, stride=sz.nl)]
+                out_refs[b][l, 8 * g : 8 * g + 8] = cells(b, l, g)
             return carry
 
         lax.fori_loop(0, sz.levels, level, 0, unroll=4)
         for k in range(HALO):
             out_refs[b][target + k] = out_refs[b][target + k] + got_ref[b, k]
+    lat = lax.axis_index("lat")
+    far = jnp.int32(KREACH)
+    for i, d in enumerate(far_of):
+        far = jnp.where(lat == i, d, far)
+    last = sz.rows // 8 - 1
+    for ref, b in zip(rim_refs, (KREACH + far, KREACH - far)):
+        for l in range(sz.levels):
+            ref[l] = cells(b, l, last)
+        for k in range(HALO):
+            ref[target + k] = ref[target + k] + got_ref[b, k, 8 * last : 8 * last + 8]
 
 
 def call(kernel, out_shape, operands, flops, smem=0, aliases=None):
@@ -259,10 +292,10 @@
     n = sz.points
     work = 2 * 192 * 256 * 256
     acc = call(functools.partial(clear_kernel, sz), shape(sz.total, cols), (), 10 * work)
-    acc, pos, wl, wr, wc, down, up = call(
+    acc, pos, wl, wr, wc, near, far = call(
         functools.partial(first_kernel, sz),
         (
-            shape(sz.total, cols), shape(3, n, cols), shape(4, n, cols),
+            shape(sz.total, cols), shape(4, n, cols), shape(4, n, cols),
             shape(4, n, cols), shape(8, n, cols),
             shape(SPAN, HALO * sz.nl, cols), shape(SPAN, HALO * sz.nl, cols),
         ),
@@ -272,59 +305,69 @@
         aliases={1: 0},
     )
 
-    def rows_by(d):
+    def pair_with(odd):
         def step(lon, lat, lev):
-            return (lon, lat + d, lev) if 0 <= lat + d < sizes[1] else None
+            to = lat + 1 if lat % 2 == odd else lat - 1
+            return (lon, to, lev) if 0 <= to < sizes[1] else None
+
         return step
 
-    got_down = permute(down, sizes, rows_by(-1))
-    got_up = permute(up, sizes, rows_by(1))
-    part = 5
-    inner_levels = levels - HALO
+    got_near = permute(near, sizes, pair_with(0))
+    got_far = permute(far, sizes, pair_with(1))
+    groups = (rows - 2 * HALO) // HALO
 
     def inner(acc, lower, upper):
         return call(
             functools.partial(inner_kernel, sz, lower, upper),
             shape(sz.total, cols),
             (shifts, acc, pos, wl, wr, wc),
-            (upper - lower) * 18 * work,
+            (upper - lower) * 39 * work,
             smem=1,
             aliases={1: 0},
         )
 
-    acc = inner(acc, 0, part)
+    acc = inner(acc, 0, groups // 2)
     acc, edge = call(
         functools.partial(row_kernel, sz),
         (shape(sz.total, cols), shape(SPAN, HALO, rows, cols)),
-        (acc, got_down, got_up),
+        (acc, got_near, got_far),
         1 << 20,
         aliases={0: 0},
     )
     got_edge = permute(edge, sizes, lambda lon, lat, lev: (lon, lat, 1 - lev))
-    acc = inner(acc, part, inner_levels)
+    acc = inner(acc, groups // 2, groups)
+    reach = [((lat + 1) * (KREACH - 1)) // sizes[1] + 1 for lat in range(sizes[1])]
+    above = reach[1:] + reach[-1:]
+    far_of = [r + 1 if nxt > r else 0 for r, nxt in zip(reach, above)]
     blocks = call(
-        functools.partial(level_kernel, sz),
-        tuple(shape(levels, rows, cols) for _ in range(SPAN)),
+        functools.partial(level_kernel, sz, far_of),
+        tuple(shape(levels, rows, cols) for _ in range(SPAN))
+        + tuple(shape(levels, 8, cols) for _ in range(2)),
         (acc, got_edge),
         1 << 20,
     )
 
-    def reach(lat):
-        return ((lat + 1) * (KREACH - 1)) // sizes[1] + 1
-
     def around(d):
         def step(lon, lat, lev):
-            far = max(reach(lat), reach(min(lat + 1, sizes[1] - 1)))
-            return ((lon + d) % sizes[0], lat, lev) if abs(d) <= far else None
+            return ((lon + d) % sizes[0], lat, lev) if abs(d) <= reach[lat] else None
+
+        return step
+
+    def rim_around(sign):
+        def step(lon, lat, lev):
+            d = sign * far_of[lat]
+            return ((lon + d) % sizes[0], lat, lev) if d else None
 
         return step
 
     total = adjoint_in + blocks[KREACH]
     order = (2, -2, 1, -1, 3, -3)
     got = [permute(blocks[KREACH + d], sizes, around(d)) for d in order]
+    rims = [permute(blocks[SPAN + i], sizes, rim_around(1 - 2 * i)) for i in range(2)]
     for value in got:
         total = total + value
-    return total
+    pads = ((0, 0), (rows - 8, 0), (0, 0))
+    return total + jnp.pad(rims[0] + rims[1], pads)
 
 
 def solution(mesh):

time: 66.7 us -> 64.7 us (0.970)
  waiting for transfers between devices: 10.1 us -> 6.31 us
  starting transfers between devices: 35.8 us -> 39.5 us
  Pallas kernels: 18.5 us -> 16.5 us
    ppermute x9 -> x11, waiting for transfers between devices: 10.1 us -> 6.31 us  [permute(): return lax.ppermute(value, AXES, pairs)]
    ppermute x9 -> x11, starting transfers between devices: 35.8 us -> 39.5 us  [permute(): return lax.ppermute(value, AXES, pairs)]
    pallas_call x6, Pallas kernels: 18.5 us -> 16.5 us  [call(): pl.pallas_call(kernel, out_shape=out_shape, in_specs=specs, out_specs=jax...]
  transfers between devices with their start and end apart: 9 -> 11, of which waited for: 4 -> 4; matrix products, arithmetic and copies ran while one was open for 0% -> 0% of each run, Pallas kernels for 15% -> 14%
where the time goes in v2:
time: 64.7 us; the launch traced here: 64.3 us
  starting transfers between devices  39.5 us (61%)
  Pallas kernels  16.5 us (26%)
  waiting for transfers between devices  6.31 us (10%)
  local copies, waits for them, and re-layouts  0.98 us (2%)
  other arithmetic  0.77 us (1%)
    ppermute x11, starting transfers between devices, permute(): return lax.ppermute(value, AXES, pairs)  39.5 us
    pallas_call x6, Pallas kernels, call(): pl.pallas_call(kernel, out_shape=out_shape, in_specs=specs, out_specs=jax...  16.5 us
    ppermute x11, waiting for transfers between devices, permute(): return lax.ppermute(value, AXES, pairs)  6.31 us
  transfers between devices with their start and end apart: 11, of which 4 were waited for; matrix products, arithmetic and copies ran while one was open for 0% of the time, Pallas kernels for 14%

profile of v2, /device:TPU:2, one launch (start us, length us, event | category | flops | bytes accessed | tf_op | source)
XLA Modules:
  0.0 64.3 jit_solution(17932275014758232318)
XLA Ops:
  0.0 0.2 shard_map.55.acc_in
  0.3 0.5 copy-done.3
  0.7 0.2 copy-done.2
  0.9 0.2 copy-done
  1.2 0.0 copy-done.1
  1.2 6.9 %shard_map.56 = (f32[5040,128]{1,0:T(8,128)S(1)}, f32[4,384,128]{2,1,0:T(8,128)S(1)}, f32[4,384,128]{2,1,0:T(8,128)S(1)}, f32[4,384,128]{2,1,0:T(8,128)S(1)}, f3...) custom-call(s32[32,24]{1,0:T(8,128)S(1)} %bitcast.1, ...), custom_call_target="tpu_custom_call", output_to_operand_aliasing={{0}: (1, {})} | custom-call | flops 3774873600 | bytes 1048576 | tf_op jit(solution)/shard_map/pallas_call | solution.py:256
  8.1 1.9 %collective-permute-start = (f32[7,72,128]{2,1,0:T(8,128)S(1)}, f32[7,72,128]{2,1,0:T(8,128)S(1)}, u32[]{:S(2)}, u32[]{:S(2)}) collective-permute-start(f32[7,72,128]{2,1,0:T(8,128)S(1)} %get-tuple-element.28), channel_id=1, source_target_pairs={{0,2},{1,3},{2,0},{3,1},{4,6},{5,7},{6,4},{7,5},{8,10},{9,11},{10,... | collective-permute-start | bytes 774152 | tf_op jit(solution)/shard_map/ppermute | solution.py:284
  10.0 7.9 %collective-permute-start.1 = (f32[7,72,128]{2,1,0:T(8,128)S(1)}, f32[7,72,128]{2,1,0:T(8,128)S(1)}, u32[]{:S(2)}, u32[]{:S(2)}) collective-permute-start(f32[7,72,128]{2,1,0:T(8,128)S(1)} %get-tuple-element.29), channel_id=1, source_target_pairs={{2,4},{3,5},{4,2},{5,3},{10,12},{11,13},{12,10},{13,11},{18,20},{1... | collective-permute-start | bytes 774152 | tf_op jit(solution)/shard_map/ppermute | solution.py:284
  18.0 4.4 %shard_map.57.acc_in = f32[5040,128]{1,0:T(8,128)S(1)} custom-call(s32[32,24]{1,0:T(8,128)S(1)} %bitcast.2, f32[5040,128]{1,0:T(8,128)S(1)} %get-tuple-element.23.acc_in, f32[4,384,128]{2,1,0:T(8,128)S(1)} %get-tuple-element.24.pos_ref, f32[4,384,128]{2,1,0:T(8,128)S(1)} %get-tuple-element.25.wl_ref, ...), custom_call_target="tpu_custom_call", output_to_operand_aliasing={{}: (1, {})} | custom-call | flops 2944401408 | bytes 1048576 | tf_op jit(solution)/shard_map/pallas_call | solution.py:256
  22.4 0.0 collective-permute-done.near_ref
  22.4 1.2 %collective-permute-done.1.far_ref = f32[7,72,128]{2,1,0:T(8,128)S(1)} collective-permute-done((f32[7,72,128]{2,1,0:T(8,128)S(1)}, f32[7,72,128]{2,1,0:T(8,128)S(1)}, u32[]{:S(2)}, u32[]{:S(2)}) %collective-permute-start.1) | collective-permute-done | bytes 258080 | tf_op jit(solution)/shard_map/ppermute | solution.py:284
  23.6 0.1 shard_map.58
  23.7 1.9 %collective-permute-start.2 = (f32[7,3,24,128]{3,2,1,0:T(8,128)S(1)}, f32[7,3,24,128]{3,2,1,0:T(8,128)S(1)}, u32[]{:S(2)}, u32[]{:S(2)}) collective-permute-start(f32[7,3,24,128]{3,2,1,0:T(8,128)S(1)} %get-tuple-element.31), channel_id=1, source_target_pairs={{0,1},{1,0},{2,3},{3,2},{4,5},{5,4},{6,7},{7,6},{8,9},{9,8},{10,11... | collective-permute-start | bytes 774152 | tf_op jit(solution)/shard_map/ppermute | solution.py:284
  25.7 4.4 %shard_map.59.acc_ref = f32[5040,128]{1,0:T(8,128)S(1)} custom-call(s32[32,24]{1,0:T(8,128)S(1)} %bitcast.3, f32[5040,128]{1,0:T(8,128)S(1)} %get-tuple-element.30.acc_in, f32[4,384,128]{2,1,0:T(8,128)S(1)} %get-tuple-element.24.pos_ref, f32[4,384,128]{2,1,0:T(8,128)S(1)} %get-tuple-element.25.wl_ref, ...), custom_call_target="tpu_custom_call", output_to_operand_aliasing={{}: (1, {})} | custom-call | flops 2944401408 | bytes 1048576 | tf_op jit(solution)/shard_map/pallas_call | solution.py:256
  30.1 0.0 copy-start.4
  30.1 3.3 %collective-permute-done.2.got_ref = f32[7,3,24,128]{3,2,1,0:T(8,128)S(1)} collective-permute-done((f32[7,3,24,128]{3,2,1,0:T(8,128)S(1)}, f32[7,3,24,128]{3,2,1,0:T(8,128)S(1)}, u32[]{:S(2)}, u32[]{:S(2)}) %collective-permute-start.2) | collective-permute-done | bytes 258080 | tf_op jit(solution)/shard_map/ppermute | solution.py:284
  33.5 0.4 shard_map.60
  33.8 1.9 %collective-permute-start.3 = (f32[16,24,128]{2,1,0:T(8,128)S(1)}, f32[16,24,128]{2,1,0:T(8,128)S(1)}, u32[]{:S(2)}, u32[]{:S(2)}) collective-permute-start(f32[16,24,128]{2,1,0:T(8,128)S(1)} %get-tuple-element.33), channel_id=1, source_target_pairs={{2,18},{3,19},{4,20},{5,21},{6,22},{7,23},{10,26},{11,27},{12,28},... | collective-permute-start | bytes 589832 | tf_op jit(solution)/shard_map/ppermute | solution.py:284
  35.8 1.9 %collective-permute-start.9 = (f32[16,8,128]{2,1,0:T(8,128)S(1)}, f32[16,8,128]{2,1,0:T(8,128)S(1)}, u32[]{:S(2)}, u32[]{:S(2)}) collective-permute-start(f32[16,8,128]{2,1,0:T(8,128)S(1)} %get-tuple-element.39), channel_id=1, source_target_pairs={{0,16},{1,17},{4,28},{5,29},{8,24},{9,25},{12,36},{13,37},{16,32},... | collective-permute-start | bytes 196616 | tf_op jit(solution)/shard_map/ppermute | solution.py:284
  37.7 8.8 %collective-permute-start.10 = (f32[16,8,128]{2,1,0:T(8,128)S(1)}, f32[16,8,128]{2,1,0:T(8,128)S(1)}, u32[]{:S(2)}, u32[]{:S(2)}) collective-permute-start(f32[16,8,128]{2,1,0:T(8,128)S(1)} %get-tuple-element.40), channel_id=1, source_target_pairs={{0,496},{1,497},{4,492},{5,493},{8,504},{9,505},{12,500},{13,501},... | collective-permute-start | bytes 196616 | tf_op jit(solution)/shard_map/ppermute | solution.py:284
  46.5 4.7 %collective-permute-start.4 = (f32[16,24,128]{2,1,0:T(8,128)S(1)}, f32[16,24,128]{2,1,0:T(8,128)S(1)}, u32[]{:S(2)}, u32[]{:S(2)}) collective-permute-start(f32[16,24,128]{2,1,0:T(8,128)S(1)} %get-tuple-element.34), channel_id=1, source_target_pairs={{2,498},{3,499},{4,500},{5,501},{6,502},{7,503},{10,506},{11,507},... | collective-permute-start | bytes 589832 | tf_op jit(solution)/shard_map/ppermute | solution.py:284
  51.1 2.6 %collective-permute-start.5 = (f32[16,24,128]{2,1,0:T(8,128)S(1)}, f32[16,24,128]{2,1,0:T(8,128)S(1)}, u32[]{:S(2)}, u32[]{:S(2)}) collective-permute-start(f32[16,24,128]{2,1,0:T(8,128)S(1)} %get-tuple-element.35), channel_id=1, source_target_pairs={{0,8},{1,9},{2,10},{3,11},{4,12},{5,13},{6,14},{7,15},{8,16},{9,17... | collective-permute-start | bytes 589832 | tf_op jit(solution)/shard_map/ppermute | solution.py:284
  53.7 6.6 %collective-permute-start.6 = (f32[16,24,128]{2,1,0:T(8,128)S(1)}, f32[16,24,128]{2,1,0:T(8,128)S(1)}, u32[]{:S(2)}, u32[]{:S(2)}) collective-permute-start(f32[16,24,128]{2,1,0:T(8,128)S(1)} %get-tuple-element.36), channel_id=1, source_target_pairs={{0,504},{1,505},{2,506},{3,507},{4,508},{5,509},{6,510},{7,511},{8... | collective-permute-start | bytes 589832 | tf_op jit(solution)/shard_map/ppermute | solution.py:284
  60.3 0.0 collective-permute-done.10
  60.3 0.7 %collective-permute-start.7 = (f32[16,24,128]{2,1,0:T(8,128)S(1)}, f32[16,24,128]{2,1,0:T(8,128)S(1)}, u32[]{:S(2)}, u32[]{:S(2)}) collective-permute-start(f32[16,24,128]{2,1,0:T(8,128)S(1)} %get-tuple-element.37), channel_id=1, source_target_pairs={{6,30},{7,31},{14,38},{15,39},{22,46},{23,47},{30,54},{31,55},{38,... | collective-permute-start | bytes 589832 | tf_op jit(solution)/shard_map/ppermute | solution.py:284
  61.0 0.0 collective-permute-done.3
  61.0 0.7 %collective-permute-start.8 = (f32[16,24,128]{2,1,0:T(8,128)S(1)}, f32[16,24,128]{2,1,0:T(8,128)S(1)}, u32[]{:S(2)}, u32[]{:S(2)}) collective-permute-start(f32[16,24,128]{2,1,0:T(8,128)S(1)} %get-tuple-element.38), channel_id=1, source_target_pairs={{6,494},{7,495},{14,502},{15,503},{22,510},{23,511},{30,6},{31,7},... | collective-permute-start | bytes 589832 | tf_op jit(solution)/shard_map/ppermute | solution.py:284
  61.7 0.0 collective-permute-done.4
  61.7 0.4 collective-permute-done.5
  62.1 1.4 %collective-permute-done.6 = f32[16,24,128]{2,1,0:T(8,128)S(1)} collective-permute-done((f32[16,24,128]{2,1,0:T(8,128)S(1)}, f32[16,24,128]{2,1,0:T(8,128)S(1)}, u32[]{:S(2)}, u32[]{:S(2)}) %collective-permute-start.6) | collective-permute-done | bytes 196640 | tf_op jit(solution)/shard_map/ppermute | solution.py:284
  63.5 0.0 collective-permute-done.7
  63.5 0.8 %pad_add_fusion = f32[16,24,128]{2,1,0:T(8,128)} fusion(f32[16,8,128]{2,1,0:T(8,128)S(1)} %add.36, f32[16,24,128]{2,1,0:T(8,128)S(1)} %collective-permute-done.8, f32[16,24,128]{2,1,0:T(8,128)S(1)} %collective-permute-done.7, f32[16,24,128]{2,1,0:T(8,128)S(1)} %collective-permute-done.6, f32[16,24,128]{2,1,0:T(8,128)S(1)} %collective-permute-done.5, ...), kind=kLoop, calls=%fused_computation | loop fusion | flops 393216 | bytes 1835008 | tf_op jit(solution)/shard_map/add | solution.py:370
  (8 shorter events, 0.0 us)
Async XLA Ops:
  0.0 0.7 %copy-start.3 = (s32[2,16,24,1]{2,3,1,0:T(1,128)S(1)}, s32[2,16,24,1]{2,3,1,0:T(1,128)}, u32[]{:S(2)}) copy-start(s32[2,16,24,1]{2,3,1,0:T(1,128)} %param.9) | copy-start | bytes 9220
  0.0 0.9 %copy-start.2 = (s32[16,24,128]{2,1,0:T(8,128)S(1)}, s32[16,24,128]{2,1,0:T(8,128)}, u32[]{:S(2)}) copy-start(s32[16,24,128]{2,1,0:T(8,128)} %base_ref.1) | copy-start | bytes 589828
  0.0 1.2 %copy-start = (f32[3,16,24,128]{3,2,1,0:T(8,128)S(1)}, f32[3,16,24,128]{3,2,1,0:T(8,128)}, u32[]{:S(2)}) copy-start(f32[3,16,24,128]{3,2,1,0:T(8,128)} %frac_ref.1) | copy-start | bytes 1769476
  0.0 1.2 %copy-start.1 = (f32[16,24,128]{2,1,0:T(8,128)S(1)}, f32[16,24,128]{2,1,0:T(8,128)}, u32[]{:S(2)}) copy-start(f32[16,24,128]{2,1,0:T(8,128)} %cot_ref.1) | copy-start | bytes 589828
  8.1 14.3 %collective-permute-start = (f32[7,72,128]{2,1,0:T(8,128)S(1)}, f32[7,72,128]{2,1,0:T(8,128)S(1)}, u32[]{:S(2)}, u32[]{:S(2)}) collective-permute-start(f32[7,72,128]{2,1,0:T(8,128)S(1)} %get-tuple-element.28), channel_id=1, source_target_pairs={{0,2},{1,3},{2,0},{3,1},{4,6},{5,7},{6,4},{7,5},{8,10},{9,11},{10,... | collective-permute-start | bytes 774152 | tf_op jit(solution)/shard_map/ppermute | solution.py:284
  10.0 13.6 %collective-permute-start.1 = (f32[7,72,128]{2,1,0:T(8,128)S(1)}, f32[7,72,128]{2,1,0:T(8,128)S(1)}, u32[]{:S(2)}, u32[]{:S(2)}) collective-permute-start(f32[7,72,128]{2,1,0:T(8,128)S(1)} %get-tuple-element.29), channel_id=1, source_target_pairs={{2,4},{3,5},{4,2},{5,3},{10,12},{11,13},{12,10},{13,11},{18,20},{1... | collective-permute-start | bytes 774152 | tf_op jit(solution)/shard_map/ppermute | solution.py:284
  23.7 9.7 %collective-permute-start.2 = (f32[7,3,24,128]{3,2,1,0:T(8,128)S(1)}, f32[7,3,24,128]{3,2,1,0:T(8,128)S(1)}, u32[]{:S(2)}, u32[]{:S(2)}) collective-permute-start(f32[7,3,24,128]{3,2,1,0:T(8,128)S(1)} %get-tuple-element.31), channel_id=1, source_target_pairs={{0,1},{1,0},{2,3},{3,2},{4,5},{5,4},{6,7},{7,6},{8,9},{9,8},{10,11... | collective-permute-start | bytes 774152 | tf_op jit(solution)/shard_map/ppermute | solution.py:284
  30.1 33.4 %copy-start.4 = (f32[16,24,128]{2,1,0:T(8,128)S(1)}, f32[16,24,128]{2,1,0:T(8,128)}, u32[]{:S(2)}) copy-start(f32[16,24,128]{2,1,0:T(8,128)} %param.5) | copy-start | bytes 589828
  33.8 27.2 %collective-permute-start.3 = (f32[16,24,128]{2,1,0:T(8,128)S(1)}, f32[16,24,128]{2,1,0:T(8,128)S(1)}, u32[]{:S(2)}, u32[]{:S(2)}) collective-permute-start(f32[16,24,128]{2,1,0:T(8,128)S(1)} %get-tuple-element.33), channel_id=1, source_target_pairs={{2,18},{3,19},{4,20},{5,21},{6,22},{7,23},{10,26},{11,27},{12,28},... | collective-permute-start | bytes 589832 | tf_op jit(solution)/shard_map/ppermute | solution.py:284
  35.8 18.0 %collective-permute-start.9 = (f32[16,8,128]{2,1,0:T(8,128)S(1)}, f32[16,8,128]{2,1,0:T(8,128)S(1)}, u32[]{:S(2)}, u32[]{:S(2)}) collective-permute-start(f32[16,8,128]{2,1,0:T(8,128)S(1)} %get-tuple-element.39), channel_id=1, source_target_pairs={{0,16},{1,17},{4,28},{5,29},{8,24},{9,25},{12,36},{13,37},{16,32},... | collective-permute-start | bytes 196616 | tf_op jit(solution)/shard_map/ppermute | solution.py:284
  37.7 22.6 %collective-permute-start.10 = (f32[16,8,128]{2,1,0:T(8,128)S(1)}, f32[16,8,128]{2,1,0:T(8,128)S(1)}, u32[]{:S(2)}, u32[]{:S(2)}) collective-permute-start(f32[16,8,128]{2,1,0:T(8,128)S(1)} %get-tuple-element.40), channel_id=1, source_target_pairs={{0,496},{1,497},{4,492},{5,493},{8,504},{9,505},{12,500},{13,501},... | collective-permute-start | bytes 196616 | tf_op jit(solution)/shard_map/ppermute | solution.py:284
  46.5 15.3 %collective-permute-start.4 = (f32[16,24,128]{2,1,0:T(8,128)S(1)}, f32[16,24,128]{2,1,0:T(8,128)S(1)}, u32[]{:S(2)}, u32[]{:S(2)}) collective-permute-start(f32[16,24,128]{2,1,0:T(8,128)S(1)} %get-tuple-element.34), channel_id=1, source_target_pairs={{2,498},{3,499},{4,500},{5,501},{6,502},{7,503},{10,506},{11,507},... | collective-permute-start | bytes 589832 | tf_op jit(solution)/shard_map/ppermute | solution.py:284
  51.1 11.0 %collective-permute-start.5 = (f32[16,24,128]{2,1,0:T(8,128)S(1)}, f32[16,24,128]{2,1,0:T(8,128)S(1)}, u32[]{:S(2)}, u32[]{:S(2)}) collective-permute-start(f32[16,24,128]{2,1,0:T(8,128)S(1)} %get-tuple-element.35), channel_id=1, source_target_pairs={{0,8},{1,9},{2,10},{3,11},{4,12},{5,13},{6,14},{7,15},{8,16},{9,17... | collective-permute-start | bytes 589832 | tf_op jit(solution)/shard_map/ppermute | solution.py:284
  53.7 9.8 %collective-permute-start.6 = (f32[16,24,128]{2,1,0:T(8,128)S(1)}, f32[16,24,128]{2,1,0:T(8,128)S(1)}, u32[]{:S(2)}, u32[]{:S(2)}) collective-permute-start(f32[16,24,128]{2,1,0:T(8,128)S(1)} %get-tuple-element.36), channel_id=1, source_target_pairs={{0,504},{1,505},{2,506},{3,507},{4,508},{5,509},{6,510},{7,511},{8... | collective-permute-start | bytes 589832 | tf_op jit(solution)/shard_map/ppermute | solution.py:284
  60.3 3.2 %collective-permute-start.7 = (f32[16,24,128]{2,1,0:T(8,128)S(1)}, f32[16,24,128]{2,1,0:T(8,128)S(1)}, u32[]{:S(2)}, u32[]{:S(2)}) collective-permute-start(f32[16,24,128]{2,1,0:T(8,128)S(1)} %get-tuple-element.37), channel_id=1, source_target_pairs={{6,30},{7,31},{14,38},{15,39},{22,46},{23,47},{30,54},{31,55},{38,... | collective-permute-start | bytes 589832 | tf_op jit(solution)/shard_map/ppermute | solution.py:284
  61.0 2.5 %collective-permute-start.8 = (f32[16,24,128]{2,1,0:T(8,128)S(1)}, f32[16,24,128]{2,1,0:T(8,128)S(1)}, u32[]{:S(2)}, u32[]{:S(2)}) collective-permute-start(f32[16,24,128]{2,1,0:T(8,128)S(1)} %get-tuple-element.38), channel_id=1, source_target_pairs={{6,494},{7,495},{14,502},{15,503},{22,510},{23,511},{30,6},{31,7},... | collective-permute-start | bytes 589832 | tf_op jit(solution)/shard_map/ppermute | solution.py:284

commit v3 on v2

--- a/solution.py
+++ b/solution.py
@@ -166,14 +166,6 @@
         return carry
 
     lax.fori_loop(0, sz.levels // 4, rims, 0)
-    edge = jnp.where(lax.axis_index("lev") == 0, sz.levels - HALO, 0)
-    inner = range(HALO, sz.rows - HALO)
-
-    def edges(i, carry):
-        add_blocks(sz, [(edge + i, j) for j in inner], acc_ref, *refs)
-        return carry
-
-    lax.fori_loop(0, HALO, edges, 0)
     n = HALO * sz.nl
     even = lax.axis_index("lat") % 2 == 0
     near = jnp.where(even, sz.rows + HALO, 0)
@@ -188,6 +180,15 @@
 ):
     refs = (shift_ref, pos_ref, wl_ref, wr_ref, wc_ref)
     start = jnp.where(lax.axis_index("lev") == 0, 0, HALO)
+    edge = jnp.where(lax.axis_index("lev") == 0, sz.levels - HALO, 0)
+    across = range(HALO, sz.rows - HALO)
+
+    def edges(i, carry):
+        add_blocks(sz, [(edge + i, j) for j in across], acc_ref, *refs)
+        return carry
+
+    if lower == 0:
+        lax.fori_loop(0, HALO, edges, 0)
     span = range(sz.levels - HALO)
 
     def rows(i, carry):
@@ -300,7 +301,7 @@
             shape(SPAN, HALO * sz.nl, cols), shape(SPAN, HALO * sz.nl, cols),
         ),
         (shifts, acc, cotangent, fraction, base_index),
-        150 * work,
+        96 * work,
         smem=1,
         aliases={1: 0},
     )
@@ -321,12 +322,12 @@
             functools.partial(inner_kernel, sz, lower, upper),
             shape(sz.total, cols),
             (shifts, acc, pos, wl, wr, wc),
-            (upper - lower) * 39 * work,
+            ((upper - lower) * 39 + (54 if lower == 0 else 0)) * work,
             smem=1,
             aliases={1: 0},
         )
 
-    acc = inner(acc, 0, groups // 2)
+    acc = inner(acc, 0, groups // 3)
     acc, edge = call(
         functools.partial(row_kernel, sz),
         (shape(sz.total, cols), shape(SPAN, HALO, rows, cols)),
@@ -335,7 +336,7 @@
         aliases={0: 0},
     )
     got_edge = permute(edge, sizes, lambda lon, lat, lev: (lon, lat, 1 - lev))
-    acc = inner(acc, groups // 2, groups)
+    acc = inner(acc, groups // 3, groups)
     reach = [((lat + 1) * (KREACH - 1)) // sizes[1] + 1 for lat in range(sizes[1])]
     above = reach[1:] + reach[-1:]
     far_of = [r + 1 if nxt > r else 0 for r, nxt in zip(reach, above)]

time: 64.7 us -> 63.3 us (0.978)
  waiting for transfers between devices: 6.31 us -> 3.93 us
  starting transfers between devices: 39.5 us -> 40.5 us
    ppermute x11, waiting for transfers between devices: 6.31 us -> 3.93 us  [permute(): return lax.ppermute(value, AXES, pairs)]
    ppermute x11, starting transfers between devices: 39.5 us -> 40.5 us  [permute(): return lax.ppermute(value, AXES, pairs)]
  transfers between devices with their start and end apart: 11 -> 11, of which waited for: 4 -> 3; matrix products, arithmetic and copies ran while one was open for 0% -> 0% of each run, Pallas kernels for 14% -> 17%
where the time goes in v3:
time: 63.3 us; the launch traced here: 62.9 us
  starting transfers between devices  40.5 us (64%)
  Pallas kernels  16.5 us (26%)
  waiting for transfers between devices  3.93 us (6%)
  local copies, waits for them, and re-layouts  0.98 us (2%)
  other arithmetic  0.77 us (1%)
    ppermute x11, starting transfers between devices, permute(): return lax.ppermute(value, AXES, pairs)  40.5 us
    pallas_call x6, Pallas kernels, call(): pl.pallas_call(kernel, out_shape=out_shape, in_specs=specs, out_specs=jax...  16.5 us
    ppermute x11, waiting for transfers between devices, permute(): return lax.ppermute(value, AXES, pairs)  3.93 us
  transfers between devices with their start and end apart: 11, of which 3 were waited for; matrix products, arithmetic and copies ran while one was open for 0% of the time, Pallas kernels for 17%

profile of v3, /device:TPU:2, one launch (start us, length us, event | category | flops | bytes accessed | tf_op | source)
XLA Modules:
  0.0 62.9 jit_solution(1280189119093333246)
XLA Ops:
  0.0 0.2 shard_map.55.acc_in
  0.3 0.5 copy-done.3
  0.7 0.2 copy-done.2
  0.9 0.2 copy-done
  1.2 0.0 copy-done.1
  1.2 4.9 %shard_map.56 = (f32[5040,128]{1,0:T(8,128)S(1)}, f32[4,384,128]{2,1,0:T(8,128)S(1)}, f32[4,384,128]{2,1,0:T(8,128)S(1)}, f32[4,384,128]{2,1,0:T(8,128)S(1)}, f3...) custom-call(s32[32,24]{1,0:T(8,128)S(1)} %bitcast.1, ...), custom_call_target="tpu_custom_call", output_to_operand_aliasing={{0}: (1, {})} | custom-call | flops 2415919104 | bytes 1048576 | tf_op jit(solution)/shard_map/pallas_call | solution.py:257
  6.1 1.9 %collective-permute-start = (f32[7,72,128]{2,1,0:T(8,128)S(1)}, f32[7,72,128]{2,1,0:T(8,128)S(1)}, u32[]{:S(2)}, u32[]{:S(2)}) collective-permute-start(f32[7,72,128]{2,1,0:T(8,128)S(1)} %get-tuple-element.28), channel_id=1, source_target_pairs={{0,2},{1,3},{2,0},{3,1},{4,6},{5,7},{6,4},{7,5},{8,10},{9,11},{10,... | collective-permute-start | bytes 774152 | tf_op jit(solution)/shard_map/ppermute | solution.py:285
  8.1 7.9 %collective-permute-start.1 = (f32[7,72,128]{2,1,0:T(8,128)S(1)}, f32[7,72,128]{2,1,0:T(8,128)S(1)}, u32[]{:S(2)}, u32[]{:S(2)}) collective-permute-start(f32[7,72,128]{2,1,0:T(8,128)S(1)} %get-tuple-element.29), channel_id=1, source_target_pairs={{2,4},{3,5},{4,2},{5,3},{10,12},{11,13},{12,10},{13,11},{18,20},{1... | collective-permute-start | bytes 774152 | tf_op jit(solution)/shard_map/ppermute | solution.py:285
  16.0 5.2 %shard_map.57.acc_in = f32[5040,128]{1,0:T(8,128)S(1)} custom-call(s32[32,24]{1,0:T(8,128)S(1)} %bitcast.2, f32[5040,128]{1,0:T(8,128)S(1)} %get-tuple-element.23.acc_in, f32[4,384,128]{2,1,0:T(8,128)S(1)} %get-tuple-element.24.pos_ref, f32[4,384,128]{2,1,0:T(8,128)S(1)} %get-tuple-element.25.wl_ref, ...), custom_call_target="tpu_custom_call", output_to_operand_aliasing={{}: (1, {})} | custom-call | flops 3321888768 | bytes 1048576 | tf_op jit(solution)/shard_map/pallas_call | solution.py:257
  21.2 0.0 collective-permute-done.near_ref
  21.2 0.0 collective-permute-done.1.far_ref
  21.2 0.1 shard_map.58
  21.4 1.9 %collective-permute-start.2 = (f32[7,3,24,128]{3,2,1,0:T(8,128)S(1)}, f32[7,3,24,128]{3,2,1,0:T(8,128)S(1)}, u32[]{:S(2)}, u32[]{:S(2)}) collective-permute-start(f32[7,3,24,128]{3,2,1,0:T(8,128)S(1)} %get-tuple-element.31), channel_id=1, source_target_pairs={{0,1},{1,0},{2,3},{3,2},{4,5},{5,4},{6,7},{7,6},{8,9},{9,8},{10,11... | collective-permute-start | bytes 774152 | tf_op jit(solution)/shard_map/ppermute | solution.py:285
  23.3 5.7 %shard_map.59.acc_ref = f32[5040,128]{1,0:T(8,128)S(1)} custom-call(s32[32,24]{1,0:T(8,128)S(1)} %bitcast.3, f32[5040,128]{1,0:T(8,128)S(1)} %get-tuple-element.30.acc_in, f32[4,384,128]{2,1,0:T(8,128)S(1)} %get-tuple-element.24.pos_ref, f32[4,384,128]{2,1,0:T(8,128)S(1)} %get-tuple-element.25.wl_ref, ...), custom_call_target="tpu_custom_call", output_to_operand_aliasing={{}: (1, {})} | custom-call | flops 3925868544 | bytes 1048576 | tf_op jit(solution)/shard_map/pallas_call | solution.py:257
  29.0 0.0 copy-start.4
  29.0 2.1 %collective-permute-done.2.got_ref = f32[7,3,24,128]{3,2,1,0:T(8,128)S(1)} collective-permute-done((f32[7,3,24,128]{3,2,1,0:T(8,128)S(1)}, f32[7,3,24,128]{3,2,1,0:T(8,128)S(1)}, u32[]{:S(2)}, u32[]{:S(2)}) %collective-permute-start.2) | collective-permute-done | bytes 258080 | tf_op jit(solution)/shard_map/ppermute | solution.py:285
  31.1 0.4 shard_map.60
  31.5 1.9 %collective-permute-start.3 = (f32[16,24,128]{2,1,0:T(8,128)S(1)}, f32[16,24,128]{2,1,0:T(8,128)S(1)}, u32[]{:S(2)}, u32[]{:S(2)}) collective-permute-start(f32[16,24,128]{2,1,0:T(8,128)S(1)} %get-tuple-element.33), channel_id=1, source_target_pairs={{2,18},{3,19},{4,20},{5,21},{6,22},{7,23},{10,26},{11,27},{12,28},... | collective-permute-start | bytes 589832 | tf_op jit(solution)/shard_map/ppermute | solution.py:285
  33.4 2.5 %collective-permute-start.9 = (f32[16,8,128]{2,1,0:T(8,128)S(1)}, f32[16,8,128]{2,1,0:T(8,128)S(1)}, u32[]{:S(2)}, u32[]{:S(2)}) collective-permute-start(f32[16,8,128]{2,1,0:T(8,128)S(1)} %get-tuple-element.39), channel_id=1, source_target_pairs={{0,16},{1,17},{4,28},{5,29},{8,24},{9,25},{12,36},{13,37},{16,32},... | collective-permute-start | bytes 196616 | tf_op jit(solution)/shard_map/ppermute | solution.py:285
  36.0 9.1 %collective-permute-start.10 = (f32[16,8,128]{2,1,0:T(8,128)S(1)}, f32[16,8,128]{2,1,0:T(8,128)S(1)}, u32[]{:S(2)}, u32[]{:S(2)}) collective-permute-start(f32[16,8,128]{2,1,0:T(8,128)S(1)} %get-tuple-element.40), channel_id=1, source_target_pairs={{0,496},{1,497},{4,492},{5,493},{8,504},{9,505},{12,500},{13,501},... | collective-permute-start | bytes 196616 | tf_op jit(solution)/shard_map/ppermute | solution.py:285
  45.1 4.7 %collective-permute-start.4 = (f32[16,24,128]{2,1,0:T(8,128)S(1)}, f32[16,24,128]{2,1,0:T(8,128)S(1)}, u32[]{:S(2)}, u32[]{:S(2)}) collective-permute-start(f32[16,24,128]{2,1,0:T(8,128)S(1)} %get-tuple-element.34), channel_id=1, source_target_pairs={{2,498},{3,499},{4,500},{5,501},{6,502},{7,503},{10,506},{11,507},... | collective-permute-start | bytes 589832 | tf_op jit(solution)/shard_map/ppermute | solution.py:285
  49.8 2.6 %collective-permute-start.5 = (f32[16,24,128]{2,1,0:T(8,128)S(1)}, f32[16,24,128]{2,1,0:T(8,128)S(1)}, u32[]{:S(2)}, u32[]{:S(2)}) collective-permute-start(f32[16,24,128]{2,1,0:T(8,128)S(1)} %get-tuple-element.35), channel_id=1, source_target_pairs={{0,8},{1,9},{2,10},{3,11},{4,12},{5,13},{6,14},{7,15},{8,16},{9,17... | collective-permute-start | bytes 589832 | tf_op jit(solution)/shard_map/ppermute | solution.py:285
  52.3 0.0 collective-permute-done.9
  52.3 6.6 %collective-permute-start.6 = (f32[16,24,128]{2,1,0:T(8,128)S(1)}, f32[16,24,128]{2,1,0:T(8,128)S(1)}, u32[]{:S(2)}, u32[]{:S(2)}) collective-permute-start(f32[16,24,128]{2,1,0:T(8,128)S(1)} %get-tuple-element.36), channel_id=1, source_target_pairs={{0,504},{1,505},{2,506},{3,507},{4,508},{5,509},{6,510},{7,511},{8... | collective-permute-start | bytes 589832 | tf_op jit(solution)/shard_map/ppermute | solution.py:285
  58.9 0.0 collective-permute-done.10
  59.0 0.7 %collective-permute-start.7 = (f32[16,24,128]{2,1,0:T(8,128)S(1)}, f32[16,24,128]{2,1,0:T(8,128)S(1)}, u32[]{:S(2)}, u32[]{:S(2)}) collective-permute-start(f32[16,24,128]{2,1,0:T(8,128)S(1)} %get-tuple-element.37), channel_id=1, source_target_pairs={{6,30},{7,31},{14,38},{15,39},{22,46},{23,47},{30,54},{31,55},{38,... | collective-permute-start | bytes 589832 | tf_op jit(solution)/shard_map/ppermute | solution.py:285
  59.6 0.0 collective-permute-done.3
  59.6 0.7 %collective-permute-start.8 = (f32[16,24,128]{2,1,0:T(8,128)S(1)}, f32[16,24,128]{2,1,0:T(8,128)S(1)}, u32[]{:S(2)}, u32[]{:S(2)}) collective-permute-start(f32[16,24,128]{2,1,0:T(8,128)S(1)} %get-tuple-element.38), channel_id=1, source_target_pairs={{6,494},{7,495},{14,502},{15,503},{22,510},{23,511},{30,6},{31,7},... | collective-permute-start | bytes 589832 | tf_op jit(solution)/shard_map/ppermute | solution.py:285
  60.3 0.0 collective-permute-done.4
  60.4 0.4 collective-permute-done.5
  60.7 1.4 %collective-permute-done.6 = f32[16,24,128]{2,1,0:T(8,128)S(1)} collective-permute-done((f32[16,24,128]{2,1,0:T(8,128)S(1)}, f32[16,24,128]{2,1,0:T(8,128)S(1)}, u32[]{:S(2)}, u32[]{:S(2)}) %collective-permute-start.6) | collective-permute-done | bytes 196640 | tf_op jit(solution)/shard_map/ppermute | solution.py:285
  62.2 0.8 %pad_add_fusion = f32[16,24,128]{2,1,0:T(8,128)} fusion(f32[16,8,128]{2,1,0:T(8,128)S(1)} %add.36, f32[16,24,128]{2,1,0:T(8,128)S(1)} %collective-permute-done.8, f32[16,24,128]{2,1,0:T(8,128)S(1)} %collective-permute-done.7, f32[16,24,128]{2,1,0:T(8,128)S(1)} %collective-permute-done.6, f32[16,24,128]{2,1,0:T(8,128)S(1)} %collective-permute-done.5, ...), kind=kLoop, calls=%fused_computation | loop fusion | flops 393216 | bytes 1835008 | tf_op jit(solution)/shard_map/add | solution.py:371
  (8 shorter events, 0.0 us)
Async XLA Ops:
  0.0 0.7 %copy-start.3 = (s32[2,16,24,1]{2,3,1,0:T(1,128)S(1)}, s32[2,16,24,1]{2,3,1,0:T(1,128)}, u32[]{:S(2)}) copy-start(s32[2,16,24,1]{2,3,1,0:T(1,128)} %param.9) | copy-start | bytes 9220
  0.0 0.9 %copy-start.2 = (s32[16,24,128]{2,1,0:T(8,128)S(1)}, s32[16,24,128]{2,1,0:T(8,128)}, u32[]{:S(2)}) copy-start(s32[16,24,128]{2,1,0:T(8,128)} %base_ref.1) | copy-start | bytes 589828
  0.0 1.2 %copy-start = (f32[3,16,24,128]{3,2,1,0:T(8,128)S(1)}, f32[3,16,24,128]{3,2,1,0:T(8,128)}, u32[]{:S(2)}) copy-start(f32[3,16,24,128]{3,2,1,0:T(8,128)} %frac_ref.1) | copy-start | bytes 1769476
  0.0 1.2 %copy-start.1 = (f32[16,24,128]{2,1,0:T(8,128)S(1)}, f32[16,24,128]{2,1,0:T(8,128)}, u32[]{:S(2)}) copy-start(f32[16,24,128]{2,1,0:T(8,128)} %cot_ref.1) | copy-start | bytes 589828
  6.1 15.1 %collective-permute-start = (f32[7,72,128]{2,1,0:T(8,128)S(1)}, f32[7,72,128]{2,1,0:T(8,128)S(1)}, u32[]{:S(2)}, u32[]{:S(2)}) collective-permute-start(f32[7,72,128]{2,1,0:T(8,128)S(1)} %get-tuple-element.28), channel_id=1, source_target_pairs={{0,2},{1,3},{2,0},{3,1},{4,6},{5,7},{6,4},{7,5},{8,10},{9,11},{10,... | collective-permute-start | bytes 774152 | tf_op jit(solution)/shard_map/ppermute | solution.py:285
  8.1 13.2 %collective-permute-start.1 = (f32[7,72,128]{2,1,0:T(8,128)S(1)}, f32[7,72,128]{2,1,0:T(8,128)S(1)}, u32[]{:S(2)}, u32[]{:S(2)}) collective-permute-start(f32[7,72,128]{2,1,0:T(8,128)S(1)} %get-tuple-element.29), channel_id=1, source_target_pairs={{2,4},{3,5},{4,2},{5,3},{10,12},{11,13},{12,10},{13,11},{18,20},{1... | collective-permute-start | bytes 774152 | tf_op jit(solution)/shard_map/ppermute | solution.py:285
  21.4 9.7 %collective-permute-start.2 = (f32[7,3,24,128]{3,2,1,0:T(8,128)S(1)}, f32[7,3,24,128]{3,2,1,0:T(8,128)S(1)}, u32[]{:S(2)}, u32[]{:S(2)}) collective-permute-start(f32[7,3,24,128]{3,2,1,0:T(8,128)S(1)} %get-tuple-element.31), channel_id=1, source_target_pairs={{0,1},{1,0},{2,3},{3,2},{4,5},{5,4},{6,7},{7,6},{8,9},{9,8},{10,11... | collective-permute-start | bytes 774152 | tf_op jit(solution)/shard_map/ppermute | solution.py:285
  29.0 33.2 %copy-start.4 = (f32[16,24,128]{2,1,0:T(8,128)S(1)}, f32[16,24,128]{2,1,0:T(8,128)}, u32[]{:S(2)}) copy-start(f32[16,24,128]{2,1,0:T(8,128)} %param.5) | copy-start | bytes 589828
  31.5 28.2 %collective-permute-start.3 = (f32[16,24,128]{2,1,0:T(8,128)S(1)}, f32[16,24,128]{2,1,0:T(8,128)S(1)}, u32[]{:S(2)}, u32[]{:S(2)}) collective-permute-start(f32[16,24,128]{2,1,0:T(8,128)S(1)} %get-tuple-element.33), channel_id=1, source_target_pairs={{2,18},{3,19},{4,20},{5,21},{6,22},{7,23},{10,26},{11,27},{12,28},... | collective-permute-start | bytes 589832 | tf_op jit(solution)/shard_map/ppermute | solution.py:285
  33.4 18.9 %collective-permute-start.9 = (f32[16,8,128]{2,1,0:T(8,128)S(1)}, f32[16,8,128]{2,1,0:T(8,128)S(1)}, u32[]{:S(2)}, u32[]{:S(2)}) collective-permute-start(f32[16,8,128]{2,1,0:T(8,128)S(1)} %get-tuple-element.39), channel_id=1, source_target_pairs={{0,16},{1,17},{4,28},{5,29},{8,24},{9,25},{12,36},{13,37},{16,32},... | collective-permute-start | bytes 196616 | tf_op jit(solution)/shard_map/ppermute | solution.py:285
  36.0 23.0 %collective-permute-start.10 = (f32[16,8,128]{2,1,0:T(8,128)S(1)}, f32[16,8,128]{2,1,0:T(8,128)S(1)}, u32[]{:S(2)}, u32[]{:S(2)}) collective-permute-start(f32[16,8,128]{2,1,0:T(8,128)S(1)} %get-tuple-element.40), channel_id=1, source_target_pairs={{0,496},{1,497},{4,492},{5,493},{8,504},{9,505},{12,500},{13,501},... | collective-permute-start | bytes 196616 | tf_op jit(solution)/shard_map/ppermute | solution.py:285
  45.1 15.3 %collective-permute-start.4 = (f32[16,24,128]{2,1,0:T(8,128)S(1)}, f32[16,24,128]{2,1,0:T(8,128)S(1)}, u32[]{:S(2)}, u32[]{:S(2)}) collective-permute-start(f32[16,24,128]{2,1,0:T(8,128)S(1)} %get-tuple-element.34), channel_id=1, source_target_pairs={{2,498},{3,499},{4,500},{5,501},{6,502},{7,503},{10,506},{11,507},... | collective-permute-start | bytes 589832 | tf_op jit(solution)/shard_map/ppermute | solution.py:285
  49.8 11.0 %collective-permute-start.5 = (f32[16,24,128]{2,1,0:T(8,128)S(1)}, f32[16,24,128]{2,1,0:T(8,128)S(1)}, u32[]{:S(2)}, u32[]{:S(2)}) collective-permute-start(f32[16,24,128]{2,1,0:T(8,128)S(1)} %get-tuple-element.35), channel_id=1, source_target_pairs={{0,8},{1,9},{2,10},{3,11},{4,12},{5,13},{6,14},{7,15},{8,16},{9,17... | collective-permute-start | bytes 589832 | tf_op jit(solution)/shard_map/ppermute | solution.py:285
  52.3 9.8 %collective-permute-start.6 = (f32[16,24,128]{2,1,0:T(8,128)S(1)}, f32[16,24,128]{2,1,0:T(8,128)S(1)}, u32[]{:S(2)}, u32[]{:S(2)}) collective-permute-start(f32[16,24,128]{2,1,0:T(8,128)S(1)} %get-tuple-element.36), channel_id=1, source_target_pairs={{0,504},{1,505},{2,506},{3,507},{4,508},{5,509},{6,510},{7,511},{8... | collective-permute-start | bytes 589832 | tf_op jit(solution)/shard_map/ppermute | solution.py:285
  59.0 3.2 %collective-permute-start.7 = (f32[16,24,128]{2,1,0:T(8,128)S(1)}, f32[16,24,128]{2,1,0:T(8,128)S(1)}, u32[]{:S(2)}, u32[]{:S(2)}) collective-permute-start(f32[16,24,128]{2,1,0:T(8,128)S(1)} %get-tuple-element.37), channel_id=1, source_target_pairs={{6,30},{7,31},{14,38},{15,39},{22,46},{23,47},{30,54},{31,55},{38,... | collective-permute-start | bytes 589832 | tf_op jit(solution)/shard_map/ppermute | solution.py:285
  59.6 2.5 %collective-permute-start.8 = (f32[16,24,128]{2,1,0:T(8,128)S(1)}, f32[16,24,128]{2,1,0:T(8,128)S(1)}, u32[]{:S(2)}, u32[]{:S(2)}) collective-permute-start(f32[16,24,128]{2,1,0:T(8,128)S(1)} %get-tuple-element.38), channel_id=1, source_target_pairs={{6,494},{7,495},{14,502},{15,503},{22,510},{23,511},{30,6},{31,7},... | collective-permute-start | bytes 589832 | tf_op jit(solution)/shard_map/ppermute | solution.py:285
